TPU v7x, 512 devices: a whole 4x4x16 slice. The times are simulated.
512 devices in a mesh: wave: 64 (over z, x), lev: 8 (over y, core).
Axes of the slice: x: 4, y: 4, z: 16, core: 2. Of those that a mesh axis runs over, the one named last changes fastest.
Arguments:
- spectra: bfloat16 [8, 1280, 8, 1280], P('lev', 'wave'), may hold values from -0.0048828125 to 0.0048828125
- wave_order: int32 [1280], replicated, may hold values from 0 to 1279, as said below
- truncation: int32 [1280], replicated, may hold values from 160 to 1280, as said below
Outputs:
- flux_spectra: float32 [8, 1280, 8, 1280], P('lev', 'wave')
Inputs may be any that keep to these rules, and one draw needn't show every extreme that they name: `wave_order`: A permutation of 0 to 1279; in each block of 20 rows the r-th row holds a wavenumber from r * (64) to (r + 1) * 64 - 1. `truncation`: equal at latitudes j and 1279 - j.
All inputs are finite; a program needn't handle non-finite values.
Results may differ from a plain program's by a relative error of at most 0.02.
Values may be sent and summed in bfloat16 or wider, within the bound.
A program may use at most 192 MiB of HBM per device.

v0:
```python
import math

import jax
import jax.numpy as jnp
from jax import lax
from jax.sharding import PartitionSpec as P

unroll_length = 64
rescale_every = 8


def diagonal_logs(top_wave):
    counts_j = jnp.arange(1, top_wave, dtype=jnp.int32).astype(jnp.float32)
    log_terms = jnp.log((2.0 * counts_j + 1.0) / (2.0 * counts_j))
    summed = jnp.concatenate([jnp.zeros((1,), jnp.float32), jnp.cumsum(log_terms)])
    return 0.5 * math.log(0.5) + 0.5 * summed


def legendre_scan(wavenums, latitudes, count_k, lat_count, top_wave, consume, init):
    log_table = diagonal_logs(top_wave)
    picker = wavenums[:, None] == jnp.arange(top_wave, dtype=jnp.int32)[None, :]
    row_logs = jnp.sum(jnp.where(picker, log_table[None, :], jnp.float32(0.0)), axis=1)
    order_m = wavenums.astype(jnp.float32)[:, None]
    angles = math.pi / lat_count * (latitudes.astype(jnp.float32) + 0.5)
    cosine = jnp.cos(angles)[None, :]
    sines = jnp.sin(angles)[None, :]
    grid_shape = (wavenums.shape[0], latitudes.shape[0])
    scale_log = row_logs[:, None] + order_m * jnp.log(sines)
    previous = jnp.zeros(grid_shape, jnp.float32)
    current = jnp.ones(grid_shape, jnp.float32)

    def advance(carry, block_index):
        previous, current, scale_log, running = carry
        outputs = []
        for unroll_step in range(unroll_length):
            degree_k = block_index * unroll_length + unroll_step
            kept_mask = wavenums[:, None] + degree_k < top_wave
            outputs.append(
                jnp.where(kept_mask, current * jnp.exp(scale_log), jnp.float32(0.0)).astype(
                    jnp.bfloat16
                )
            )
            next_k = (degree_k + 1).astype(jnp.float32)
            degree = order_m + next_k
            coef_alpha = jnp.sqrt((4.0 * degree * degree - 1.0) / (next_k * (degree + order_m)))
            lower_degree = degree - 1.0
            coef_beta = jnp.sqrt(
                (next_k - 1.0)
                * (next_k - 1.0 + 2.0 * order_m)
                / jnp.maximum(4.0 * lower_degree * lower_degree - 1.0, 1.0)
            )
            fresh_value = coef_alpha * (cosine * current - coef_beta * previous)
            previous, current = (current, fresh_value)
            if unroll_step % rescale_every == rescale_every - 1:
                rescale = jnp.maximum(jnp.abs(previous), jnp.abs(current))
                previous = previous / rescale
                current = current / rescale
                scale_log = scale_log + jnp.log(rescale)
        running, emitted = consume(running, jnp.stack(outputs), block_index)
        return ((previous, current, scale_log, running), emitted)

    block_ids = jnp.arange(count_k // unroll_length, dtype=jnp.int32)
    carried, stacked = lax.scan(advance, (previous, current, scale_log, init), block_ids)
    return (carried[3], stacked)


def legendre_table(wavenums, latitudes, count_k, lat_count, top_wave):

    def keep_block(running, block, block_index):
        return (running, block)

    unused, stacked = legendre_scan(
        wavenums, latitudes, count_k, lat_count, top_wave, keep_block, jnp.zeros((), jnp.float32)
    )
    return stacked.reshape(count_k, wavenums.shape[0], latitudes.shape[0])


def make_dft(wavenums, lon_count):
    phases = wavenums[:, None] * jnp.arange(lon_count, dtype=jnp.int32)[None, :] % lon_count
    angles = phases.astype(jnp.float32) * (2.0 * math.pi / lon_count)
    wave_factor = jnp.where(wavenums == 0, 1.0, 2.0).astype(jnp.float32)[:, None]
    return jnp.stack([wave_factor * jnp.cos(angles), -wave_factor * jnp.sin(angles)]).astype(
        jnp.bfloat16
    )


def direct_factor(wavenums, band_lats, kept_mask, lat_count, lon_count, top_wave):
    angles = math.pi / lat_count * (band_lats.astype(jnp.float32) + 0.5)
    lat_weight = float(top_wave) / lon_count * (math.pi / lat_count * jnp.sin(angles))
    wave_factor = jnp.where(wavenums == 0, 1.0, 2.0).astype(jnp.float32)
    return jnp.where(
        kept_mask, lat_weight[None, :] / (wave_factor * wave_factor)[:, None], jnp.float32(0.0)
    )


def grid_section(banded, wavenums, band_lats, truncation, dft_table, lat_count):
    lev_dev, top_wave, comp_count, band_size = banded.shape
    field_count = comp_count // 2
    lon_count = dft_table.shape[2]
    picker = band_lats[:, None] == jnp.arange(lat_count, dtype=jnp.int32)[None, :]
    band_trunc = jnp.sum(jnp.where(picker, truncation[None, :], 0), axis=1)
    kept_mask = wavenums[:, None] < band_trunc[None, :]
    masked = (
        banded.reshape(lev_dev, top_wave, 2, field_count, band_size)
        * kept_mask.astype(jnp.bfloat16)[None, :, None, None, :]
    )
    grid_values = jnp.einsum(
        "liafj,aix->lfjx", masked, dft_table, preferred_element_type=jnp.float32
    )
    fluxes = jnp.stack(
        [
            grid_values[:, 0] * grid_values[:, 2],
            grid_values[:, 1] * grid_values[:, 2],
            grid_values[:, 0] * grid_values[:, 3],
            grid_values[:, 1] * grid_values[:, 3],
        ],
        axis=1,
    ).astype(jnp.bfloat16)
    raw_terms = jnp.einsum("lfjx,aix->liafj", fluxes, dft_table, preferred_element_type=jnp.float32)
    factor = direct_factor(wavenums, band_lats, kept_mask, lat_count, lon_count, top_wave)
    return (
        (raw_terms * factor[None, :, None, None, :])
        .reshape(lev_dev, top_wave, comp_count, band_size)
        .astype(jnp.bfloat16)
    )


def on_device(spectra, wave_order, truncation):
    lev_dev, row_count, comp_count, count_k = spectra.shape
    top_wave = wave_order.shape[0]
    lat_count = truncation.shape[0]
    wave_count = lax.axis_size("wave")
    lev_count = lax.axis_size("lev")
    band_size = lat_count // wave_count
    lat_group = lat_count // lev_count
    wave_idx = lax.axis_index("wave")
    lev_idx = lax.axis_index("lev")
    own_waves = lax.dynamic_slice_in_dim(wave_order, wave_idx * row_count, row_count)
    own_lats = lev_idx * lat_group + jnp.arange(lat_group, dtype=jnp.int32)
    band_lats = wave_idx * band_size + jnp.arange(band_size, dtype=jnp.int32)
    dft_table = make_dft(wave_order, 2 * top_wave)
    legendre = legendre_table(own_waves, own_lats, count_k, lat_count, top_wave)
    fourier = jnp.einsum(
        "lick,kip->licp",
        lax.all_gather(spectra, "lev", axis=0, tiled=True),
        legendre,
        preferred_element_type=jnp.float32,
    ).astype(jnp.bfloat16)
    banded = lax.all_to_all(
        lax.all_to_all(fourier, "lev", split_axis=0, concat_axis=3, tiled=True),
        "wave",
        split_axis=3,
        concat_axis=1,
        tiled=True,
    )
    back = grid_section(banded, wave_order, band_lats, truncation, dft_table, lat_count)
    returned = lax.all_to_all(
        lax.all_to_all(back, "wave", split_axis=1, concat_axis=3, tiled=True),
        "lev",
        split_axis=3,
        concat_axis=0,
        tiled=True,
    )
    coeff_block = lax.slice_in_dim(returned, 0, lax.axis_size("lev") * lev_dev, axis=0)
    return lax.psum_scatter(
        jnp.einsum(
            "licp,kip->lick", coeff_block, legendre, preferred_element_type=jnp.float32
        ).astype(jnp.bfloat16),
        "lev",
        scatter_dimension=0,
        tiled=True,
    ).astype(jnp.float32)


def solution(mesh):
    return jax.shard_map(
        on_device,
        mesh=mesh,
        in_specs=(P("lev", "wave", None, None), P(), P()),
        out_specs=P("lev", "wave", None, None),
        check_vma=False,
    )
```

profile of v0, /device:TPU:1, one launch (start us, length us, event | category | flops | bytes accessed | tf_op | source)
XLA Modules:
  0.0 547.5 jit_solution(15267795856210320569)
XLA Ops:
  6.5 0.7 all-gather.2.cloned.1.call-update
  7.4 0.8 convert_bitcast_fusion
  9.1 184.4 %while.20 = (s32[]{:T(128)}, f32[20,160]{1,0:T(8,128)S(1)}, f32[20,160]{1,0:T(8,128)S(1)}, f32[20,160]{1,0:T(8,128)S(1)}, bf16[20,64,20,160]{3,2,1,0:T(8,128)(2,...) while((s32[]{:T(128)}, f32[20,160]{1,0:T(8,128)S(1)}, ...), condition=%wide.region_4.5_spmd.clone, body=%wide.region_3.4_spmd.clone.sunk | while | flops 2339635 | bytes 8752688 | solution.py:63
  9.1 0.6 dynamic_slice.15
  17.4 0.9 bitcast_dynamic-update-slice_fusion.2
  18.3 0.6 dynamic_slice.15
  26.6 1.0 bitcast_dynamic-update-slice_fusion.2
  35.8 0.9 bitcast_dynamic-update-slice_fusion.2
  45.0 1.0 bitcast_dynamic-update-slice_fusion.2
  46.0 0.6 dynamic_slice.15
  54.2 0.9 bitcast_dynamic-update-slice_fusion.2
  63.4 1.0 bitcast_dynamic-update-slice_fusion.2
  64.4 0.6 dynamic_slice.15
  72.7 1.0 bitcast_dynamic-update-slice_fusion.2
  73.7 0.6 dynamic_slice.15
  82.0 0.9 bitcast_dynamic-update-slice_fusion.2
  91.2 0.9 bitcast_dynamic-update-slice_fusion.2
  100.4 0.9 bitcast_dynamic-update-slice_fusion.2
  101.3 0.6 dynamic_slice.15
  109.6 0.9 bitcast_dynamic-update-slice_fusion.2
  110.5 0.6 dynamic_slice.15
  118.8 1.0 bitcast_dynamic-update-slice_fusion.2
  128.0 0.9 bitcast_dynamic-update-slice_fusion.2
  137.2 1.0 bitcast_dynamic-update-slice_fusion.2
  146.5 1.0 bitcast_dynamic-update-slice_fusion.2
  155.7 1.0 bitcast_dynamic-update-slice_fusion.2
  164.9 0.9 bitcast_dynamic-update-slice_fusion.2
  174.1 1.0 bitcast_dynamic-update-slice_fusion.2
  183.3 0.9 bitcast_dynamic-update-slice_fusion.2
  192.5 0.9 bitcast_dynamic-update-slice_fusion.2
  193.5 18.5 %copy.69 = bf16[1280,20,160,1]{0,2,3,1:T(8,128)(2,1)} copy(bf16[1280,20,160,1]{2,1,0,3:T(8,128)(2,1)} %bitcast.1717) | data formatting | bytes 16384000 | tf_op jit(solution)/shard_map/reshape | solution.py:75
  212.3 0.7 compare_select_fusion
  213.0 7.1 %fusion.675 = bf16[8,20,8,160]{3,2,0,1:T(8,128)(2,1)S(1)} fusion(bf16[1280,20,160,1]{0,2,3,1:T(8,128)(2,1)} %copy.69, bf16[8,20,8,1280]{3,2,0,1:T(8,128)(2,1)} %all-gather.2.cloned.1.call-done), kind=kOutput, calls=%fused_computation.1204 | convolution fusion | flops 524492800 | bytes 11878400 | tf_op jit(solution)/shard_map/lick,kip->licp/dot_general | solution.py:143
  220.1 0.9 copy.52
  221.0 10.3 %all-to-all-start = ((bf16[8,20,8,160]{3,2,1,0:T(8,128)(2,1)}), bf16[8,20,8,160]{3,2,1,0:T(8,128)(2,1)S(1)}, u32[]{:S(2)}, u32[]{:S(2)}) async-start(bf16[8,20,8,160]{3,2,1,0:T(8,128)(2,1)} %copy.52), calls=%async_computation | async-start | bytes 1310720 | tf_op jit(solution)/shard_map/all_to_all | solution.py:150
  231.4 10.8 %all-to-all-done = bf16[8,20,8,160]{3,2,1,0:T(8,128)(2,1)S(1)} async-done(((bf16[8,20,8,160]{3,2,1,0:T(8,128)(2,1)}), bf16[8,20,8,160]{3,2,1,0:T(8,128)(2,1)S(1)}, u32[]{:S(2)}, u32[]{:S(2)}) %all-to-all-start) | async-done | bytes 409632 | tf_op jit(solution)/shard_map/all_to_all | solution.py:150
  242.2 3.0 copy.74
  245.1 4.2 reshape.3629
  249.3 13.9 %all-to-all-start.1 = ((bf16[64,2,1600]{2,1,0:T(2,128)(2,1)}), bf16[64,2,1600]{2,1,0:T(2,128)(2,1)S(1)}, u32[]{:S(2)}, u32[]{:S(2)}) async-start(bf16[64,2,1600]{2,1,0:T(2,128)(2,1)} %reshape.3629), calls=%async_computation.1 | async-start | bytes 851968 | tf_op jit(solution)/shard_map/all_to_all | solution.py:149
  263.2 10.9 %all-reduce.4.cloned.1.call-start = ((), (), s32[]{:S(2)}) async-start(), calls=%async_computation.5 | async-start | bytes 6553600
  274.1 58.1 %multiply_convert_fusion.1 = (bf16[1,1280,2560]{2,1,0:T(8,128)(2,1)}, bf16[1,1280,2560]{2,1,0:T(8,128)(2,1)}) fusion(s32[1280]{0:T(1024)S(1)} %copy-done, f32[1280]{0:T(1024)S(1)} %get-tuple-element.935, f32[1280]{0:T(1024)S(1)} %get-tuple-element.934), kind=kLoop, calls=%fused_computation.1192 | loop fusion | flops 42598400 | bytes 13122560 | tf_op jit(solution)/shard_map/convert.8
  332.2 3.8 reshape.3630
  336.0 6.6 %copy.75 = bf16[1,20,8,64,20]{4,3,2,1,0:T(8,128)(2,1)} copy(bf16[1,20,8,64,20]{1,2,4,3,0:T(8,128)(2,1)S(1)} %bitcast.1719) | data formatting | bytes 819200 | tf_op jit(solution)/shard_map/all_to_all | solution.py:149
  342.7 7.4 %copy.56 = bf16[1,64,20,8,20]{2,1,3,4,0:T(8,128)(2,1)S(1)} copy(bf16[1,64,20,8,20]{4,1,3,2,0:T(8,128)(2,1)} %bitcast.1720) | data formatting | bytes 819200 | tf_op jit(solution)/shard_map/all_to_all | solution.py:149
  350.1 6.0 %reshape.3618 = bf16[1280,2,4,20]{0,2,1,3:T(4,128)(2,1)S(1)} reshape(bf16[1,64,20,8,20]{2,1,3,4,0:T(8,128)(2,1)S(1)} %copy.56) | data formatting | bytes 819200 | tf_op jit(solution)/shard_map/reshape | solution.py:104
  356.4 6.2 %fusion.662 = f32[1,4,20,2560]{3,2,1,0:T(8,128)S(1)} fusion(bf16[1,1280,2560]{2,1,0:T(8,128)(2,1)} %get-tuple-element.937, bf16[1,1280,2560]{2,1,0:T(8,128)(2,1)} %get-tuple-element.936, bf16[1280,2,4,20]{0,2,1,3:T(4,128)(2,1)S(1)} %broadcast_multiply_fusion), kind=kOutput, calls=%fused_computation.1198 | convolution fusion | flops 1055129600 | bytes 14336000 | tf_op jit(solution)/shard_map/liafj,aix->lfjx/dot_general | solution.py:107
  362.7 0.7 slice-done.2
  363.4 0.7 slice-done.1
  364.1 0.7 slice-done.3
  364.8 4.1 fusion.672
  368.9 1.9 copy.58
  370.8 3.5 reshape.3631
  374.4 39.0 %all_to_all.69 = bf16[64,2,1600]{2,1,0:T(2,128)(2,1)S(1)} all-to-all(bf16[64,2,1600]{2,1,0:T(2,128)(2,1)S(1)} %reshape.3631), channel_id=1, replica_groups=mesh['wave'=64,'lev'=8] {'wave'}, dimensions={0} | all-to-all | bytes 819200 | tf_op jit(solution)/shard_map/all_to_all | solution.py:158
  413.4 3.8 reshape.3632
  417.1 6.6 %copy.76 = bf16[1,64,20,8,20]{2,1,3,4,0:T(8,128)(2,1)} copy(bf16[1,64,20,8,20]{4,3,2,1,0:T(8,128)(2,1)S(1)} %bitcast.1722) | data formatting | bytes 819200 | tf_op jit(solution)/shard_map/all_to_all | solution.py:158
  423.8 3.4 copy.77
  427.2 5.9 %reshape.3633 = bf16[8,2,12800]{2,1,0:T(2,128)(2,1)S(1)} reshape(bf16[1280,1,8,20]{3,2,1,0:T(8,128)(2,1)S(1)} %bitcast.1724) | data formatting | bytes 819200
  433.1 15.9 %all_to_all.70 = bf16[8,2,12800]{2,1,0:T(2,128)(2,1)S(1)} all-to-all(bf16[8,2,12800]{2,1,0:T(2,128)(2,1)S(1)} %reshape.3633), channel_id=1, replica_groups=mesh['wave'=64,'lev'=8] {'lev'}, dimensions={0} | all-to-all | bytes 819200 | tf_op jit(solution)/shard_map/all_to_all | solution.py:157
  449.0 6.7 %reshape.3634 = bf16[1280,1,8,20]{3,2,1,0:T(8,128)(2,1)S(1)} reshape(bf16[8,2,12800]{2,1,0:T(2,128)(2,1)S(1)} %all_to_all.70) | data formatting | bytes 819200
  455.7 2.9 copy.63
  458.7 6.3 %fusion.665 = bf16[8,20,8,1280]{3,2,0,1:T(8,128)(2,1)} fusion(bf16[1280,20,160,1]{0,2,3,1:T(8,128)(2,1)} %copy.69, bf16[1,20,8,8,160]{4,2,3,1,0:T(8,128)(2,1)S(1)} %copy.63), kind=kOutput, calls=%fused_computation.1199 | convolution fusion | flops 525926400 | bytes 11878400 | tf_op jit(solution)/shard_map/licp,kip->lick/dot_general | solution.py:166
  465.0 1.3 dynamic-slice
  466.3 71.4 %all-reduce.4.cloned.1.call-done = bf16[8,20,8,1280]{3,2,0,1:T(8,128)(2,1)} async-done(((bf16[8,20,8,1280]{3,2,0,1:T(8,128)(2,1)}), bf16[8,20,8,1280]{3,2,0,1:T(8,128)(2,1)}) %all-reduce.4.cloned.1.call-update) | async-done | bytes 3276816
  537.7 2.6 bitcast_convert_fusion
  (1613 shorter events, 138.9 us)
Async XLA Ops:
  6.5 206.4 %all-gather.2.cloned.1.call-start = ((), (), s32[]{:S(2)}) async-start(), calls=%async_computation.4 | async-start | bytes 3686400 | tf_op jit(solution)/shard_map/all_gather | solution.py:145
  193.5 18.6 %copy-start.2 = (s32[1280]{0:T(1024)S(1)}, s32[1280]{0:T(1024)}, u32[]{:S(2)}) copy-start(s32[1280]{0:T(1024)} %param.7) | copy-start | bytes 15364
  193.5 18.8 %copy-start = (s32[1280]{0:T(1024)S(1)}, s32[1280]{0:T(1024)}, u32[]{:S(2)}) copy-start(s32[1280]{0:T(1024)} %param.6) | copy-start | bytes 15364
  221.0 21.2 %all-to-all-start = ((bf16[8,20,8,160]{3,2,1,0:T(8,128)(2,1)}), bf16[8,20,8,160]{3,2,1,0:T(8,128)(2,1)S(1)}, u32[]{:S(2)}, u32[]{:S(2)}) async-start(bf16[8,20,8,160]{3,2,1,0:T(8,128)(2,1)} %copy.52), calls=%async_computation | async-start | bytes 1310720 | tf_op jit(solution)/shard_map/all_to_all | solution.py:150
  249.3 82.9 %all-to-all-start.1 = ((bf16[64,2,1600]{2,1,0:T(2,128)(2,1)}), bf16[64,2,1600]{2,1,0:T(2,128)(2,1)S(1)}, u32[]{:S(2)}, u32[]{:S(2)}) async-start(bf16[64,2,1600]{2,1,0:T(2,128)(2,1)} %reshape.3629), calls=%async_computation.1 | async-start | bytes 851968 | tf_op jit(solution)/shard_map/all_to_all | solution.py:149
  263.2 274.4 %all-reduce.4.cloned.1.call-start = ((), (), s32[]{:S(2)}) async-start(), calls=%async_computation.5 | async-start | bytes 6553600
  356.1 6.6 %slice-start = ((s8[6553600]{0:T(1024)(128)(4,1)}), s8[4194304]{0:T(1024)(128)(4,1)S(1)}, s32[]{:S(2)}) async-start(s8[6553600]{0:T(1024)(128)(4,1)} %bitcast.1726), calls=%async_computation.6 | async-start | bytes 8388608
  356.2 7.2 %slice-start.2 = ((s8[6553600]{0:T(1024)(128)(4,1)}), s8[4194304]{0:T(1024)(128)(4,1)S(1)}, s32[]{:S(2)}) async-start(s8[6553600]{0:T(1024)(128)(4,1)} %bitcast.1728), calls=%async_computation.8 | async-start | bytes 8388608
  356.4 7.8 %slice-start.1 = ((s8[6553600]{0:T(1024)(128)(4,1)}), s8[2359296]{0:T(1024)(128)(4,1)S(1)}, s32[]{:S(2)}) async-start(s8[6553600]{0:T(1024)(128)(4,1)} %bitcast.1726), calls=%async_computation.7 | async-start | bytes 4718592
  356.4 8.4 %slice-start.3 = ((s8[6553600]{0:T(1024)(128)(4,1)}), s8[2359296]{0:T(1024)(128)(4,1)S(1)}, s32[]{:S(2)}) async-start(s8[6553600]{0:T(1024)(128)(4,1)} %bitcast.1728), calls=%async_computation.9 | async-start | bytes 4718592
  356.4 8.4 %copy-start.1 = (f32[1280,20]{0,1:T(8,128)S(1)}, f32[1280,20]{0,1:T(8,128)}, u32[]{:S(2)}) copy-start(f32[1280,20]{0,1:T(8,128)} %compare_select_fusion) | copy-start | bytes 307204
Sparse Core Ops, SparseCore 0:
  9.5 41.8 all-gather.1
  465.1 72.5 all-reduce.3
where the time goes:
time: 556 us; the launch traced here: 547 us
  other arithmetic  193 us (35%)
  local copies, waits for them, and re-layouts  121 us (22%)
  waiting for transfers between devices  83 us (15%)
  blocking collectives  54.9 us (10%)
  starting transfers between devices  35.1 us (6%)
  matrix products  23.7 us (4%)
  loops' own time  23.6 us (4%)
  between operations  14 us (3%)
    while x1260, other arithmetic  111 us
    unnamed x3, waiting for transfers between devices  72.1 us
    another operation x4, other arithmetic  58.5 us
    all_to_all x1, blocking collectives, on_device(): lax.all_to_all(back, 'wave', split_axis=1, concat_axis=3, tiled=True)  39 us
    unnamed x21, local copies, waits for them, and re-layouts  31.2 us
    another operation x1, loops' own time, legendre_scan(): lax.scan(advance, (previous, current, scale_log, init), block_ids)  23.6 us
    dynamic_update_slice x20, local copies, waits for them, and re-layouts, legendre_scan(): lax.scan(advance, (previous, current, scale_log, init), block_ids)  19.1 us
    reshape x1, local copies, waits for them, and re-layouts, legendre_table(): return stacked.reshape(count_k, wavenums.shape[0], latitudes.shape[0])  18.5 us
  transfers between devices with their start and end apart: 4, of which 2 were waited for; matrix products, arithmetic and copies ran while one was open for 44% of the time, Pallas kernels for 0%

commit v1 on v0

v1 whole, which is shorter than its diff:
```python
import functools
import math

import jax
import jax.numpy as jnp
from jax import lax
from jax.experimental import pallas as pl
from jax.experimental.pallas import tpu as pltpu
from jax.sharding import PartitionSpec as P

MESH = pl.DeviceIdType.MESH
F32 = jnp.float32
BF16 = jnp.bfloat16

TOP = 1280
LON = 2560
ROWS = 20
ROWS_PAD = 24
WAVES = 64
LEVS = 8
LANES = 128
RESCALE = 16
GROUPS = ROWS // 2
WIDTHS = tuple(TOP - LANES * g for g in range(GROUPS))
TAB_LEN = (1280, 768, 256)
TAB_STRIDE = (1288, 776, 264)
COLS = WAVES * ROWS_PAD
XROWS = 672
XPAD = 768
XBLK = 112
JBLK = 8


def iota(shape, dim):
    return lax.broadcasted_iota(jnp.int32, shape, dim)


def first_latitude(lev):
    return 64 * lev + jnp.where(lev >= 6, 64, 0)


def half_angles(lat0):
    lat = iota((8, LANES), 1) + lat0
    return math.pi / TOP * (lat.astype(F32) + 0.5)


def own_orders(wo_ref, base):
    rows = iota((ROWS_PAD, LANES), 0)
    orders = jnp.full((ROWS_PAD, LANES), TOP, jnp.int32)
    for r in range(ROWS):
        orders = jnp.where(rows == r, wo_ref[base + r], orders)
    return orders


def recurrence_start(orders, lat0, alpha_ref, both_ref):
    place = iota((16, LANES), 0) * LANES + iota((16, LANES), 1)
    j = jnp.maximum(place, 1).astype(F32)
    terms = jnp.where((place >= 1) & (place < TOP), jnp.log((2.0 * j + 1.0) / (2.0 * j)), 0.0)
    rows = iota((ROWS_PAD, LANES), 0)
    logs = jnp.zeros((ROWS_PAD, LANES), F32)
    for r in range(ROWS):
        part = jnp.where(place <= orders[r : r + 1, 0:1], terms, 0.0)
        total = jnp.sum(jnp.sum(part, axis=0, keepdims=True), axis=1, keepdims=True)
        logs = jnp.where(rows == r, total, logs)
    order = orders.astype(F32)
    angles = half_angles(lat0)
    cosine = jnp.cos(angles)
    log_sine = jnp.log(jnp.sin(angles))
    for kb in range(TOP // LANES):
        k = iota((ROWS_PAD, LANES), 1) + (kb * LANES + 1)
        kf = k.astype(F32)
        n = order + kf
        alpha = jnp.sqrt((4.0 * n * n - 1.0) / (kf * (n + order)))
        low = n - 1.0
        beta = jnp.sqrt(
            (kf - 1.0) * (kf - 1.0 + 2.0 * order) / jnp.maximum(4.0 * low * low - 1.0, 1.0)
        )
        kept = orders + k < TOP
        alpha_ref[kb] = jnp.where(kept, alpha, 0.0)
        both_ref[kb] = jnp.where(kept, alpha * beta, 0.0)
    state = []
    for g in range(3):
        part = slice(8 * g, 8 * g + 8)
        scale = 0.5 * math.log(0.5) + 0.5 * logs[part] + order[part] * log_sine
        state += [jnp.zeros((8, LANES), F32), jnp.ones((8, LANES), F32), scale]
    return cosine, state


def recurrence_phase(phase, cosine, state, alpha_ref, both_ref, tabs):
    live, start, stop = ((3, 0, 2), (2, 2, 6), (1, 6, 10))[phase]

    def block(kb, flat):
        st = [tuple(flat[3 * g : 3 * g + 3]) for g in range(live)]
        alpha = alpha_ref[kb]
        both = both_ref[kb]
        for i in range(LANES):
            if i % RESCALE == 0:
                factor = [jnp.exp(s[2]) for s in st]
            for g in range(live):
                prev, cur, scale = st[g]
                rows = pl.ds(kb * LANES + i, 8, stride=TAB_STRIDE[g])
                tabs[g][rows, :] = cur * factor[g]
                part = slice(8 * g, 8 * g + 8)
                fresh = (alpha[part, i : i + 1] * cosine) * cur - both[part, i : i + 1] * prev
                st[g] = (cur, fresh, scale)
            if i % RESCALE == RESCALE - 1:
                for g in range(live):
                    prev, cur, scale = st[g]
                    big = jnp.maximum(jnp.maximum(jnp.abs(prev), jnp.abs(cur)), 1e-30)
                    inv = 1.0 / big
                    st[g] = (prev * inv, cur * inv, scale + jnp.log(big))
        return tuple(v for s in st for v in s)

    return list(lax.fori_loop(start, stop, block, tuple(state[: 3 * live])))


def table_rows(tabs, r, width):
    g = r // 8
    return tabs[g][pl.ds((r % 8) * TAB_STRIDE[g], width), :].astype(BF16)


def sin_cos(phase):
    turns = jnp.floor(phase * (1.0 / LON))
    phase = phase - turns * LON
    quarter = jnp.floor(phase * (4.0 / LON) + 0.5)
    t = (phase - quarter * (LON // 4)) * (2.0 * math.pi / LON)
    t2 = t * t
    s = t * (1.0 + t2 * (-1.0 / 6 + t2 * (1.0 / 120 + t2 * (-1.0 / 5040 + t2 * (1.0 / 362880)))))
    c = 1.0 + t2 * (-0.5 + t2 * (1.0 / 24 + t2 * (-1.0 / 720 + t2 * (1.0 / 40320))))
    odd = (quarter == 1.0) | (quarter == 3.0)
    sine = jnp.where(odd, c, s)
    cosine = jnp.where(odd, s, c)
    sine = jnp.where((quarter == 2.0) | (quarter == 3.0), -sine, sine)
    cosine = jnp.where((quarter == 1.0) | (quarter == 2.0), -cosine, cosine)
    return sine, cosine


def longitude_tables(mj_ref, cos_xj, sin_xj, cos_jx, sin_jx, even_ref):
    for jb in range(COLS // LANES):
        cols = pl.ds(jb * LANES, LANES)
        mj = mj_ref[:, cols]
        mf = mj.astype(F32)
        live = mj >= 0
        sb, cb = sin_cos(mf * iota((32, LANES), 0).astype(F32))
        sa, ca = sin_cos(mf * (32 * iota((24, LANES), 0)).astype(F32))
        sb = jnp.where(live, sb, 0.0)
        cb = jnp.where(live, cb, 0.0)
        for xa in range(XPAD // 32):
            rows = pl.ds(32 * xa, 32)
            if xa > 20:
                cos_xj[rows, cols] = jnp.zeros((32, LANES), BF16)
                sin_xj[rows, cols] = jnp.zeros((32, LANES), BF16)
                continue
            sa1, ca1 = sa[xa : xa + 1], ca[xa : xa + 1]
            c = ca1 * cb - sa1 * sb
            s = sa1 * cb + ca1 * sb
            if xa == 20:
                c = jnp.where(iota((32, LANES), 0) == 0, c, 0.0)
                s = jnp.where(iota((32, LANES), 0) == 0, s, 0.0)
            cos_xj[rows, cols] = c.astype(BF16)
            sin_xj[rows, cols] = s.astype(BF16)
        even = jnp.where(lax.rem(mj, 2) == 0, 1.0, 0.0)
        even_ref[cols, :] = jnp.broadcast_to(even, (LANES, LANES)).T
        for xb in range(XPAD // LANES):
            rows = pl.ds(xb * LANES, LANES)
            cos_jx[cols, rows] = cos_xj[rows, cols].T
            sin_jx[cols, rows] = sin_xj[rows, cols].T


def pick_fields():
    row, col = iota((256, 512), 0), iota((256, 512), 1)
    slot, s, l, part, field = row // 128, row // 64 % 2, row // 8 % 8, row // 4 % 2, row % 4
    c_part, side, c_slot = col // 256, col // 128 % 2, col // 64 % 2
    flux, c_s, c_l = col // 16 % 4, col // 8 % 2, col % 8
    wanted = jnp.where(side == 0, flux % 2, 2 + flux // 2)
    same = (slot == c_slot) & (s == c_s) & (l == c_l) & (part == c_part) & (field == wanted)
    return jnp.where(same, 1.0, 0.0).astype(BF16)


def place_fluxes():
    row, col = iota((256, 256), 0), iota((256, 256), 1)
    part, slot, flux, s, l = row // 128, row // 64 % 2, row // 16 % 4, row // 8 % 2, row % 8
    same = (slot == col // 128) & (s == col // 64 % 2) & (l == col // 8 % 8)
    same = same & (part == col // 4 % 2) & (flux == col % 4)
    return jnp.where(same, 1.0, 0.0).astype(BF16)


def kernel(
    wo_ref, trunc_ref, mj_ref, spec_ref, out_ref,
    alpha_ref, both_ref, tab0, tab1, tab2,
    cos_xj, sin_xj, cos_jx, sin_jx, even_ref,
    gath, stage, send_f, recv_f, send_b, recv_b,
    x_re, x_im, h_c, h_s,
    partial, e1_recv, e2_send, e2_recv,
    own_sem, g_send, g_recv, c_send, c_recv, f_ss, f_rs, b_ss, b_rs, e1_ss, e1_rs, e2_ss, e2_rs,
):
    me = lax.axis_index("wave")
    lev = lax.axis_index("lev")
    y = lev // 2
    core = lev % 2
    partner = y * 2 + (1 - core)
    two = (lev == 5) | (lev == 7)
    tabs = (tab0, tab1, tab2)

    recv_f[...] = jnp.zeros_like(recv_f)
    recv_b[...] = jnp.zeros_like(recv_b)

    barrier = pltpu.get_barrier_semaphore()

    @pl.loop(1, WAVES)
    def _(i):
        pl.semaphore_signal(
            barrier, inc=1, device_id=(lax.rem(me + i, WAVES), lev), device_id_type=MESH
        )

    for i in range(1, 4):
        pl.semaphore_signal(
            barrier, inc=1, device_id=(me, lax.rem(lev + 2 * i, LEVS)), device_id_type=MESH
        )
    pl.semaphore_signal(barrier, inc=1, device_id=(me, partner), device_id_type=MESH)

    longitude_tables(mj_ref, cos_xj, sin_xj, cos_jx, sin_jx, even_ref)
    lat0 = first_latitude(lev)
    orders = own_orders(wo_ref, me * ROWS)
    cosine, state = recurrence_start(orders, lat0, alpha_ref, both_ref)

    pl.semaphore_wait(barrier, WAVES - 1 + 4)

    def piece(ref, level, g):
        return ref.at[level, pl.ds(2 * g, 2), :, pl.ds(0, WIDTHS[g])]

    def own_copy():
        return pltpu.make_async_copy(spec_ref.at[0], gath.at[lev], own_sem)

    def y_copy(i, g):
        return pltpu.make_async_remote_copy(
            piece(spec_ref, 0, g), piece(gath, lev, g), g_send.at[i, g], g_recv.at[i, g],
            device_id=(me, lax.rem(lev + 2 * i, LEVS)), device_id_type=MESH,
        )

    def core_copy(i, g):
        level = lax.rem(lev + LEVS - 2 * i, LEVS)
        src = piece(spec_ref, 0, g) if i == 0 else piece(gath, level, g)
        return pltpu.make_async_remote_copy(
            src, piece(gath, level, g), c_send.at[i, g], c_recv.at[i, g],
            device_id=(me, partner), device_id_type=MESH,
        )

    own_copy().start()
    for g in range(GROUPS):
        for i in range(1, 4):
            y_copy(i, g).start()
    for g in range(GROUPS):
        core_copy(0, g).start()

    state = recurrence_phase(0, cosine, state, alpha_ref, both_ref, tabs)
    state = recurrence_phase(1, cosine, state, alpha_ref, both_ref, tabs)
    for g in range(GROUPS):
        for i in range(1, 4):
            y_copy(i, g).wait()
            core_copy(i, g).start()
    recurrence_phase(2, cosine, state, alpha_ref, both_ref, tabs)
    own_copy().wait()
    for g in range(GROUPS):
        for i in range(4):
            core_copy(i, g).wait()

    angles = half_angles(lat0)[0:1]
    unit = lat0 // 64
    low_row = trunc_ref[pl.ds(unit // 2, 1), :]
    high_row = trunc_ref[pl.ds(unit // 2 + 1, 1), :]
    split = jnp.concatenate([low_row[:, 64:], high_row[:, :64]], axis=1)
    cut = jnp.where(unit % 2 == 0, low_row, split)
    area = (float(TOP) / LON) * (math.pi / TOP) * jnp.sin(angles)
    sign = jnp.where(iota((1, TOP), 1) % 2 == 0, 1.0, -1.0)

    stage[...] = jnp.zeros_like(stage)
    for r in range(ROWS):
        width = WIDTHS[r // 2]
        table = table_rows(tabs, r, width)
        coeff = gath[:, r, :, 0:width].astype(F32).reshape(64, width)
        both_signs = jnp.concatenate([coeff, coeff * sign[:, :width]], axis=0).astype(BF16)
        fourier = jnp.dot(both_signs, table, preferred_element_type=F32)
        order = wo_ref[me * ROWS + r]
        weight = jnp.where(order == 0, 1.0, 2.0)
        fourier = fourier * jnp.where(order < cut, weight, 0.0)
        stage[pl.ds(r, LANES, stride=ROWS_PAD), :] = fourier.T

    def f_copy(i, count):
        to = lax.rem(me + i, WAVES)
        return pltpu.make_async_remote_copy(
            send_f.at[to, pl.ds(0, count)], recv_f.at[me, pl.ds(0, count)], f_ss.at[i], f_rs.at[i],
            device_id=(to, lev), device_id_type=MESH,
        )

    def b_copy(i, count):
        to = lax.rem(me + i, WAVES)
        return pltpu.make_async_remote_copy(
            send_b.at[to, pl.ds(0, count)], recv_b.at[me, pl.ds(0, count)], b_ss.at[i], b_rs.at[i],
            device_id=(to, lev), device_id_type=MESH,
        )

    def each_width(act):
        @pl.when(two)
        def _():
            act(2)

        @pl.when(jnp.logical_not(two))
        def _():
            act(1)

    @pl.loop(0, WAVES)
    def _(i):
        to = lax.rem(me + i, WAVES)
        for slot in range(2):
            rows = pl.ds(pl.multiple_of((slot * WAVES + to) * ROWS_PAD, 8), ROWS_PAD)
            send_f[to, slot] = stage[rows, :].astype(BF16)

        @pl.when(i > 0)
        def _():
            each_width(lambda count: f_copy(i, count).start())

    recv_f[me] = send_f[me]

    h_c[pl.ds(XROWS, XPAD - XROWS), :] = jnp.zeros((XPAD - XROWS, 256), BF16)
    h_s[pl.ds(XROWS, XPAD - XROWS), :] = jnp.zeros((XPAD - XROWS, 256), BF16)

    @pl.loop(1, WAVES)
    def _(i):
        each_width(lambda count: f_copy(i, count).wait())

    fields = pick_fields()

    @pl.loop(0, WAVES // JBLK)
    def _(b):
        rows = pl.ds(pl.multiple_of(b * JBLK * ROWS_PAD, 64), JBLK * ROWS_PAD)
        raw = recv_f[pl.ds(b * JBLK, JBLK)].astype(F32)
        flat = [raw[:, slot].reshape(JBLK * ROWS_PAD, LANES) for slot in range(2)]
        raw = jnp.concatenate(flat, axis=1).astype(BF16)
        picked = jnp.dot(raw, fields, preferred_element_type=F32)
        even = even_ref[rows, :]
        even = jnp.concatenate([even, even], axis=1)
        for part, ref in ((0, x_re), (1, x_im)):
            both = picked[:, 256 * part : 256 * part + 256]
            evens = both * even
            ref[rows, :] = jnp.concatenate([evens, both - evens], axis=1).astype(BF16)

    @pl.loop(0, XROWS // XBLK)
    def _(b):
        rows = pl.ds(pl.multiple_of(b * XBLK, 16), XBLK)
        c = jnp.dot(cos_xj[rows, :], x_re[...], preferred_element_type=F32)
        s = jnp.dot(sin_xj[rows, :], x_im[...], preferred_element_type=F32)
        c_sum, c_dif = c[:, :256] + c[:, 256:], c[:, :256] - c[:, 256:]
        s_sum, s_dif = s[:, :256] + s[:, 256:], s[:, :256] - s[:, 256:]

        def flux(g):
            return g[:, :128] * g[:, 128:]

        x = iota((XBLK, LANES), 0) + b * XBLK
        once = jnp.where((x == 0) | (x == LON // 4), 0.5, 1.0)
        f1 = flux(c_sum - s_sum) * once
        f2 = flux(c_sum + s_sum) * once
        f3 = flux(c_dif + s_dif) * once
        f4 = flux(c_dif - s_dif) * once
        near, far = f1 + f2, f3 + f4
        near_d, far_d = f2 - f1, f3 - f4
        h_c[rows, :] = jnp.concatenate([near + far, near - far], axis=1).astype(BF16)
        h_s[rows, :] = jnp.concatenate([near_d + far_d, near_d - far_d], axis=1).astype(BF16)

    places = place_fluxes()

    @pl.loop(0, WAVES // JBLK)
    def _(b):
        block = lax.rem(me // JBLK + b, WAVES // JBLK)
        rows = pl.ds(pl.multiple_of(block * JBLK * ROWS_PAD, 64), JBLK * ROWS_PAD)
        c = jnp.dot(cos_jx[rows, :], h_c[...], preferred_element_type=F32)
        s = jnp.dot(sin_jx[rows, :], h_s[...], preferred_element_type=F32)
        even = even_ref[rows, :] > 0.5
        c = jnp.where(even, c[:, :128], c[:, 128:])
        s = jnp.where(even, s[:, :128], s[:, 128:])
        back = jnp.dot(
            jnp.concatenate([c, s], axis=1).astype(BF16), places, preferred_element_type=F32
        )
        for slot in range(2):
            part = back[:, 128 * slot : 128 * slot + 128].reshape(JBLK, ROWS_PAD, LANES)
            send_b[pl.ds(block * JBLK, JBLK), slot] = part.astype(BF16)

        @pl.loop(0, JBLK)
        def _(n):
            to = block * JBLK + n
            i = lax.rem(to - me + WAVES, WAVES)

            @pl.when(i > 0)
            def _():
                each_width(lambda count: b_copy(i, count).start())

    recv_b[me] = send_b[me]

    @pl.loop(1, WAVES)
    def _(i):
        each_width(lambda count: b_copy(i, count).wait())

    @pl.loop(0, WAVES)
    def _(w):
        for slot in range(2):
            rows = pl.ds(pl.multiple_of((slot * WAVES + w) * ROWS_PAD, 8), ROWS_PAD)
            stage[rows, :] = recv_b[w, slot].astype(F32)

    def e1_copy(g):
        window = (slice(None), pl.ds(2 * g, 2), slice(None), pl.ds(0, WIDTHS[g]))
        return pltpu.make_async_remote_copy(
            partial.at[(1 - core,) + window], e1_recv.at[window], e1_ss.at[g], e1_rs.at[g],
            device_id=(me, partner), device_id_type=MESH,
        )

    def e2_copy(i, g):
        to_y = lax.rem(y + i, 4)
        return pltpu.make_async_remote_copy(
            piece(e2_send, to_y, g), piece(e2_recv, y, g), e2_ss.at[i, g], e2_rs.at[i, g],
            device_id=(me, to_y * 2 + core), device_id_type=MESH,
        )

    def forward(g):
        e1_copy(g).wait()
        for r in (2 * g, 2 * g + 1):
            for q in range(4):
                mine = partial[core, q, r, :, 0 : WIDTHS[g]].astype(F32)
                other = e1_recv[q, r, :, 0 : WIDTHS[g]].astype(F32)
                e2_send[q, r, :, 0 : WIDTHS[g]] = (mine + other).astype(BF16)
        for i in range(1, 4):
            e2_copy(i, g).start()

    for g in range(GROUPS):
        width = WIDTHS[g]
        for r in (2 * g, 2 * g + 1):
            table = table_rows(tabs, r, width)
            order = wo_ref[me * ROWS + r]
            weight = jnp.where(order == 0, 1.0, 0.5)
            factor = jnp.where(order < cut, area * weight, 0.0)
            back = stage[pl.ds(r, LANES, stride=ROWS_PAD), :].T * factor
            sums = lax.dot_general(
                back.astype(BF16), table, (((1,), (1,)), ((), ())), preferred_element_type=F32
            )
            sums = sums[:64] + sums[64:] * sign[:, :width]
            for l in range(LEVS):
                partial[l % 2, l // 2, r, :, 0:width] = sums[8 * l : 8 * l + 8].astype(BF16)
        e1_copy(g).start()
        if g > 0:
            forward(g - 1)
    forward(GROUPS - 1)
    for g in range(GROUPS):
        width = WIDTHS[g]
        for i in range(1, 4):
            e2_copy(i, g).wait()
        for r in (2 * g, 2 * g + 1):
            total = e2_send[y, r, :, 0:width].astype(F32)
            for i in range(1, 4):
                total = total + e2_recv[lax.rem(y + i, 4), r, :, 0:width].astype(F32)
            out_ref[0, r, :, 0:width] = total
            if width < TOP:
                out_ref[0, r, :, width:TOP] = jnp.zeros((8, TOP - width), F32)


def on_device(spectra, wave_order, truncation):
    mj = jnp.pad(wave_order.reshape(WAVES, ROWS), ((0, 0), (0, ROWS_PAD - ROWS)), constant_values=-1)
    vmem = pl.BlockSpec(memory_space=pltpu.VMEM)
    dma = pltpu.SemaphoreType.DMA
    return pl.pallas_call(
        kernel,
        out_shape=jax.ShapeDtypeStruct((1, ROWS, 8, TOP), F32),
        in_specs=[
            pl.BlockSpec(memory_space=pltpu.SMEM), vmem, vmem, pl.BlockSpec(memory_space=pl.ANY),
        ],
        out_specs=vmem,
        scratch_shapes=[
            pltpu.VMEM((10, ROWS_PAD, LANES), F32),
            pltpu.VMEM((10, ROWS_PAD, LANES), F32),
            pltpu.VMEM((8 * TAB_STRIDE[0], LANES), F32),
            pltpu.VMEM((8 * TAB_STRIDE[1], LANES), F32),
            pltpu.VMEM((8 * TAB_STRIDE[2], LANES), F32),
            pltpu.VMEM((XPAD, COLS), BF16),
            pltpu.VMEM((XPAD, COLS), BF16),
            pltpu.VMEM((COLS, XPAD), BF16),
            pltpu.VMEM((COLS, XPAD), BF16),
            pltpu.VMEM((COLS, LANES), F32),
            pltpu.VMEM((LEVS, ROWS, 8, TOP), BF16),
            pltpu.VMEM((2 * COLS, LANES), F32),
            pltpu.VMEM((WAVES, 2, ROWS_PAD, LANES), BF16),
            pltpu.VMEM((WAVES, 2, ROWS_PAD, LANES), BF16),
            pltpu.VMEM((WAVES, 2, ROWS_PAD, LANES), BF16),
            pltpu.VMEM((WAVES, 2, ROWS_PAD, LANES), BF16),
            pltpu.VMEM((COLS, 512), BF16),
            pltpu.VMEM((COLS, 512), BF16),
            pltpu.VMEM((XPAD, 256), BF16),
            pltpu.VMEM((XPAD, 256), BF16),
            pltpu.VMEM((2, 4, ROWS, 8, TOP), BF16),
            pltpu.VMEM((4, ROWS, 8, TOP), BF16),
            pltpu.VMEM((4, ROWS, 8, TOP), BF16),
            pltpu.VMEM((4, ROWS, 8, TOP), BF16),
            dma,
            dma((4, GROUPS)), dma((4, GROUPS)), dma((4, GROUPS)), dma((4, GROUPS)),
            dma((WAVES,)), dma((WAVES,)), dma((WAVES,)), dma((WAVES,)),
            dma((GROUPS,)), dma((GROUPS,)), dma((4, GROUPS)), dma((4, GROUPS)),
        ],
        compiler_params=pltpu.CompilerParams(
            collective_id=0, has_side_effects=True, vmem_limit_bytes=60 * 2**20
        ),
        name="flux_transform",
    )(wave_order, truncation.reshape(10, LANES), mj.reshape(1, COLS), spectra)


def solution(mesh):
    return jax.shard_map(
        on_device,
        mesh=mesh,
        in_specs=(P("lev", "wave", None, None), P(), P()),
        out_specs=P("lev", "wave", None, None),
        check_vma=False,
    )
```

time: 556 us -> 123 us (0.22); the launches traced: 547 us -> 122 us
  other arithmetic: 193 us -> 0 us
  Pallas kernels: 0 us -> 119 us
  local copies, waits for them, and re-layouts: 121 us -> 3.57 us
  waiting for transfers between devices: 83 us -> 0 us
  blocking collectives: 54.9 us -> 0 us
  starting transfers between devices: 35.1 us -> 0 us
  matrix products: 23.7 us -> 0 us
  loops' own time: 23.6 us -> 0 us
  between operations: 14 us -> 0.02 us
    pallas_call x0 -> x1, Pallas kernels: none -> 119 us  [on_device(): pl.pallas_call(kernel, out_shape=jax.ShapeDtypeStruct((1, ROWS, 8, TOP),...]
    while x1260 -> x0, other arithmetic: 111 us -> none
    unnamed x3 -> x0, waiting for transfers between devices: 72.1 us -> none
    another operation x25 -> x0, other arithmetic: 60.3 us -> none
    all_to_all x2 -> x0, blocking collectives: 54.9 us -> none  [the longest x1 39 us: on_device(): lax.all_to_all(back, 'wave', split_axis=1, concat_axis=3, tiled=True)]
    all_to_all x6 -> x0, local copies, waits for them, and re-layouts: 30 us -> none  [the longest x2 14.1 us: on_device(): lax.all_to_all(lax.all_to_all(fourier, 'lev', split_axis=0, concat_axis=3...]
    unnamed x21 -> x1, local copies, waits for them, and re-layouts: 31.2 us -> 2.09 us
    all_to_all x2 -> x0, starting transfers between devices: 24.2 us -> none  [the longest x1 13.9 us: on_device(): lax.all_to_all(lax.all_to_all(fourier, 'lev', split_axis=0, concat_axis=3...]
  transfers between devices with their start and end apart: 4 -> 0, of which waited for: 2 -> 0; matrix products, arithmetic and copies ran while one was open for 44% -> 0% of each run, Pallas kernels for 0% -> 0%
where the time goes in v1:
time: 123 us; the launch traced here: 122 us
  Pallas kernels  119 us (97%)
  local copies, waits for them, and re-layouts  3.57 us (3%)
    pallas_call x1, Pallas kernels, on_device(): pl.pallas_call(kernel, out_shape=jax.ShapeDtypeStruct((1, ROWS, 8, TOP),...  119 us

profile of v1, /device:TPU:1, one launch (start us, length us, event | category | flops | bytes accessed | tf_op | source)
XLA Modules:
  0.0 122.4 jit_solution(14985014145149853075)
XLA Ops:
  0.0 0.8 reshape.10
  0.8 0.7 reshape.11.mj_ref
  1.5 118.8 %flux_transform.1 = f32[1,20,8,1280]{3,2,1,0:T(8,128)} custom-call(s32[1280]{0:T(1024)} %wo_ref.1, s32[10,128]{1,0:T(8,128)} %bitcast.1, s32[1,1536]{1,0:T(1,128)} %reshape.11.mj_ref, bf16[1,20,8,1280]{3,2,1,0:T(8,128)(2,1)} %spec_ref.1), custom_call_target="tpu_custom_call" | custom-call | tf_op jit(solution)/shard_map/flux_transform/pallas_call | solution.py:468
  120.3 2.1 %copy.5 = f32[1,20,8,1280]{3,2,1,0:T(8,128)} copy(f32[1,20,8,1280]{3,2,1,0:T(8,128)} %flux_transform.1) | data formatting | bytes 1638400
  (1 shorter events, 0.0 us)

commit v2 on v1

v2 whole, which is shorter than its diff:
```python
import functools
import math

import jax
import jax.numpy as jnp
from jax import lax
from jax.experimental import pallas as pl
from jax.experimental.pallas import tpu as pltpu
from jax.sharding import PartitionSpec as P

MESH = pl.DeviceIdType.MESH
F32 = jnp.float32
BF16 = jnp.bfloat16

TOP = 1280
LON = 2560
ROWS = 20
ROWS_PAD = 24
LIGHT = 12
HEAVY = 8
WAVES = 64
LEVS = 8
LANES = 128
RESCALE = 16
GROUPS = ROWS // 2
WIDTHS = tuple(TOP - LANES * g for g in range(GROUPS))
TAB_LEN = (1280, 768, 256)
TAB_STRIDE = (1288, 776, 264)
COLS = WAVES * ROWS
LIGHT_COLS = WAVES * LIGHT
XROWS = 672
XPAD = 768
XBLK = 112
TILE = 4
UP = (0, 3, 4, 7, 8)


def iota(shape, dim):
    return lax.broadcasted_iota(jnp.int32, shape, dim)


def first_latitude(lev):
    return 160 * (lev // 2) + 64 * (lev % 2)


def half_angles(lat0):
    lat = iota((8, LANES), 1) + lat0
    return math.pi / TOP * (lat.astype(F32) + 0.5)


def own_orders(wo_ref, base):
    rows = iota((ROWS_PAD, LANES), 0)
    orders = jnp.full((ROWS_PAD, LANES), TOP, jnp.int32)
    for r in range(ROWS):
        orders = jnp.where(rows == r, wo_ref[base + r], orders)
    return orders


def recurrence_start(wo_ref, base, orders, lat0, alpha_ref, both_ref):
    place = iota((16, LANES), 0) * LANES + iota((16, LANES), 1)
    j = jnp.maximum(place, 1).astype(F32)
    terms = jnp.where((place >= 1) & (place < TOP), jnp.log((2.0 * j + 1.0) / (2.0 * j)), 0.0)
    rows = iota((ROWS_PAD, LANES), 0)
    logs = jnp.zeros((ROWS_PAD, LANES), F32)
    for r in range(ROWS):
        part = jnp.where(place <= wo_ref[base + r], terms, 0.0)
        total = jnp.sum(jnp.sum(part, axis=0, keepdims=True), axis=1, keepdims=True)
        logs = jnp.where(rows == r, total, logs)
    order = orders.astype(F32)
    angles = half_angles(lat0)
    cosine = jnp.cos(angles)
    log_sine = jnp.log(jnp.sin(angles))
    for kb in range(TOP // LANES):
        k = iota((ROWS_PAD, LANES), 1) + (kb * LANES + 1)
        kf = k.astype(F32)
        n = order + kf
        alpha = jnp.sqrt((4.0 * n * n - 1.0) / (kf * (n + order)))
        low = n - 1.0
        beta = jnp.sqrt(
            (kf - 1.0) * (kf - 1.0 + 2.0 * order) / jnp.maximum(4.0 * low * low - 1.0, 1.0)
        )
        kept = orders + k < TOP
        alpha_ref[kb] = jnp.where(kept, alpha, 0.0)
        both_ref[kb] = jnp.where(kept, alpha * beta, 0.0)
    state = []
    for g in range(3):
        part = slice(8 * g, 8 * g + 8)
        scale = 0.5 * math.log(0.5) + 0.5 * logs[part] + order[part] * log_sine
        state += [jnp.zeros((8, LANES), F32), jnp.ones((8, LANES), F32), scale]
    return cosine, state


def recurrence_phase(phase, cosine, state, alpha_ref, both_ref, tabs):
    live, start, stop = ((3, 0, 2), (2, 2, 6), (1, 6, 10))[phase]

    def block(kb, flat):
        st = [tuple(flat[3 * g : 3 * g + 3]) for g in range(live)]
        alpha = alpha_ref[kb]
        both = both_ref[kb]
        for i in range(LANES):
            if i % RESCALE == 0:
                factor = [jnp.exp(s[2]) for s in st]
            for g in range(live):
                prev, cur, scale = st[g]
                rows = pl.ds(kb * LANES + i, 8, stride=TAB_STRIDE[g])
                tabs[g][rows, :] = cur * factor[g]
                part = slice(8 * g, 8 * g + 8)
                fresh = (alpha[part, i : i + 1] * cosine) * cur - both[part, i : i + 1] * prev
                st[g] = (cur, fresh, scale)
            if i % RESCALE == RESCALE - 1:
                for g in range(live):
                    prev, cur, scale = st[g]
                    big = jnp.maximum(jnp.maximum(jnp.abs(prev), jnp.abs(cur)), 1e-30)
                    inv = 1.0 / big
                    st[g] = (prev * inv, cur * inv, scale + jnp.log(big))
        return tuple(v for s in st for v in s)

    return list(lax.fori_loop(start, stop, block, tuple(state[: 3 * live])))


def table_rows(tabs, r, width):
    g = r // 8
    return tabs[g][pl.ds((r % 8) * TAB_STRIDE[g], width), :].astype(BF16)


def sin_cos(phase):
    turns = jnp.floor(phase * (1.0 / LON))
    phase = phase - turns * LON
    quarter = jnp.floor(phase * (4.0 / LON) + 0.5)
    t = (phase - quarter * (LON // 4)) * (2.0 * math.pi / LON)
    t2 = t * t
    s = t * (1.0 + t2 * (-1.0 / 6 + t2 * (1.0 / 120 + t2 * (-1.0 / 5040 + t2 * (1.0 / 362880)))))
    c = 1.0 + t2 * (-0.5 + t2 * (1.0 / 24 + t2 * (-1.0 / 720 + t2 * (1.0 / 40320))))
    odd = (quarter == 1.0) | (quarter == 3.0)
    sine = jnp.where(odd, c, s)
    cosine = jnp.where(odd, s, c)
    sine = jnp.where((quarter == 2.0) | (quarter == 3.0), -sine, sine)
    cosine = jnp.where((quarter == 1.0) | (quarter == 2.0), -cosine, cosine)
    return sine, cosine


def longitude_tables(mt_ref, cos_xj, sin_xj, cos_jx, sin_jx, even_ref):
    @pl.loop(0, COLS // LANES)
    def _(jb):
        cols = pl.ds(pl.multiple_of(jb * LANES, LANES), LANES)
        mj = mt_ref[pl.ds(jb, 1), :]
        mf = mj.astype(F32)
        sb, cb = sin_cos(mf * iota((32, LANES), 0).astype(F32))
        sa, ca = sin_cos(mf * (32 * iota((24, LANES), 0)).astype(F32))
        for xa in range(XPAD // 32):
            rows = pl.ds(32 * xa, 32)
            if xa > 20:
                cos_xj[rows, cols] = jnp.zeros((32, LANES), BF16)
                sin_xj[rows, cols] = jnp.zeros((32, LANES), BF16)
                continue
            sa1, ca1 = sa[xa : xa + 1], ca[xa : xa + 1]
            c = ca1 * cb - sa1 * sb
            s = sa1 * cb + ca1 * sb
            if xa == 20:
                c = jnp.where(iota((32, LANES), 0) == 0, c, 0.0)
                s = jnp.where(iota((32, LANES), 0) == 0, s, 0.0)
            cos_xj[rows, cols] = c.astype(BF16)
            sin_xj[rows, cols] = s.astype(BF16)
        even = jnp.where(lax.rem(mj, 2) == 0, 1.0, 0.0)
        even_ref[cols, :] = jnp.broadcast_to(even, (LANES, LANES)).T
        for xb in range(XPAD // LANES):
            rows = pl.ds(xb * LANES, LANES)
            cos_jx[cols, rows] = cos_xj[rows, cols].T
            sin_jx[cols, rows] = sin_xj[rows, cols].T


def grid_lane(u):
    slot, v = u // 64, u % 64
    flux = jnp.where(slot == 0, v // 16, v // 8)
    s = jnp.where(slot == 0, v // 8 % 2, v // 4 % 2)
    level = jnp.where(slot == 0, v % 8, v % 4)
    return slot, flux, s, level, (slot == 0) | (v < 32)


def pick_fields():
    row, col = iota((256, 512), 0), iota((256, 512), 1)
    slot, level, s, part, field = row // 128, row // 16 % 8, row // 8 % 2, row // 4 % 2, row % 4
    c_part, side = col // 256, col // 128 % 2
    c_slot, flux, c_s, c_level, used = grid_lane(col % 128)
    wanted = jnp.where(side == 0, flux % 2, 2 + flux // 2)
    same = used & (slot == c_slot) & (s == c_s) & (level == c_level)
    same = same & (part == c_part) & (field == wanted)
    return jnp.where(same, 1.0, 0.0).astype(BF16)


def place_fluxes():
    row, col = iota((256, 256), 0), iota((256, 256), 1)
    part = row // 128
    slot, flux, s, level, used = grid_lane(row % 128)
    c_slot = col // 128
    c_level = jnp.where(c_slot == 0, col // 16 % 8, col // 16 % 4)
    same = used & (slot == c_slot) & (level == c_level) & (s == col // 8 % 2)
    same = same & (part == col // 4 % 2) & (flux == col % 4)
    return jnp.where(same, 1.0, 0.0).astype(BF16)


def kernel(
    wo_ref, mt_ref, spec_ref, out_ref,
    alpha_ref, both_ref, tab0, tab1, tab2,
    cos_xj, sin_xj, cos_jx, sin_jx, even_ref,
    gath, stage_l, stage_h, send_fl, send_fh, recv_fl, recv_fh, send_bl, send_bh, recv_bl, recv_bh,
    flat0, flat1, x_re, x_im, acc_c, acc_s, h_c, h_s,
    partial, e1_recv, e2_send, e2_sum, rel_recv, e2_recv,
    own_sem, g_send, g_recv, r_send, r_recv, c_send, c_recv,
    fl_ss, fl_rs, fh_ss, fh_rs, bl_ss, bl_rs, bh_ss, bh_rs,
    e1_ss, e1_rs, rel_ss, rel_rs, e2_ss, e2_rs, sum_ss, sum_rs,
):
    me = lax.axis_index("wave")
    lev = lax.axis_index("lev")
    y = lev // 2
    core = lev % 2
    partner = y * 2 + (1 - core)
    up = lax.rem(lev + 2, LEVS)
    down = lax.rem(lev + 6, LEVS)
    tabs = (tab0, tab1, tab2)
    lane4 = iota((TILE, LANES), 1)

    barrier = pltpu.get_barrier_semaphore()
    for other in (up, down, partner):
        pl.semaphore_signal(barrier, inc=1, device_id=(me, other), device_id_type=MESH)

    @pl.loop(1, WAVES)
    def _(i):
        pl.semaphore_signal(
            barrier, inc=1, device_id=(lax.rem(me + i, WAVES), lev), device_id_type=MESH
        )

    lat0 = first_latitude(lev)
    orders = own_orders(wo_ref, me * ROWS)
    cosine, state = recurrence_start(wo_ref, me * ROWS, orders, lat0, alpha_ref, both_ref)
    flat0[...] = jnp.zeros_like(flat0)
    flat1[...] = jnp.zeros_like(flat1)
    h_c[pl.ds(XROWS, XPAD - XROWS), :] = jnp.zeros((XPAD - XROWS, 256), BF16)
    h_s[pl.ds(XROWS, XPAD - XROWS), :] = jnp.zeros((XPAD - XROWS, 256), BF16)

    longitude_tables(mt_ref, cos_xj, sin_xj, cos_jx, sin_jx, even_ref)
    pl.semaphore_wait(barrier, WAVES - 1 + 3)

    light_groups = tuple(range(HEAVY // 2, GROUPS))
    heavy_groups = tuple(range(HEAVY // 2))

    def piece(ref, level, g):
        return ref.at[level, pl.ds(2 * g, 2), :, pl.ds(0, WIDTHS[g])]

    def own_copy():
        return pltpu.make_async_copy(spec_ref.at[0], gath.at[lev], own_sem)

    def y_copy(way, g):
        return pltpu.make_async_remote_copy(
            piece(spec_ref, 0, g), piece(gath, lev, g), g_send.at[way, g], g_recv.at[way, g],
            device_id=(me, up if way == 0 else down), device_id_type=MESH,
        )

    def relay_copy(g):
        level = down if g in UP else up
        return pltpu.make_async_remote_copy(
            piece(gath, level, g), piece(gath, level, g), r_send.at[g], r_recv.at[g],
            device_id=(me, up if g in UP else down), device_id_type=MESH,
        )

    def core_copy(i, g):
        level = (lev, down, up, lax.rem(lev + 4, LEVS))[i]
        src = piece(spec_ref, 0, g) if i == 0 else piece(gath, level, g)
        return pltpu.make_async_remote_copy(
            src, piece(gath, level, g), c_send.at[i, g], c_recv.at[i, g],
            device_id=(me, partner), device_id_type=MESH,
        )

    def pass_on(groups):
        for g in groups:
            for way in range(2):
                y_copy(way, g).wait()
            relay_copy(g).start()
            for i in (1, 2):
                core_copy(i, g).start()

    def pass_last(groups):
        for g in groups:
            relay_copy(g).wait()
            core_copy(3, g).start()

    def gathered(groups):
        for g in groups:
            for i in range(4):
                core_copy(i, g).wait()

    for g in light_groups + heavy_groups:
        for way in range(2):
            y_copy(way, g).start()
    own_copy().start()
    for g in light_groups + heavy_groups:
        core_copy(0, g).start()

    angles = half_angles(lat0)[0:1]
    unit = lat0 // 32
    cut_row = COLS // LANES + unit // 4
    wide = jnp.concatenate([mt_ref[pl.ds(cut_row, 1), :], mt_ref[pl.ds(cut_row + 1, 1), :]], axis=1)
    cut = wide[:, 0:LANES]
    for n in range(1, 4):
        cut = jnp.where(unit % 4 == n, wide[:, 32 * n : 32 * n + LANES], cut)
    area = (float(TOP) / LON) * (math.pi / TOP) * jnp.sin(angles)
    area = jnp.where(iota((1, LANES), 1) < 64 + 32 * core, area, 0.0)
    sign = jnp.where(iota((1, TOP), 1) % 2 == 0, 1.0, -1.0)

    def legendre_row(r):
        width = WIDTHS[r // 2]
        table = table_rows(tabs, r, width)
        coeff = gath[:, r, :, 0:width].astype(F32)
        both_signs = jnp.stack([coeff, coeff * sign[:, :width]], axis=1).reshape(LANES, width)
        fourier = jnp.dot(both_signs.astype(BF16), table, preferred_element_type=F32)
        order = wo_ref[me * ROWS + r]
        weight = jnp.where(order == 0, 1.0, 2.0)
        fourier = fourier * jnp.where(order < cut, weight, 0.0)
        if r < HEAVY:
            stage_h[pl.ds(r, LANES, stride=HEAVY), :] = fourier.T
        else:
            stage_l[pl.ds(r - HEAVY, LANES, stride=LIGHT), :] = fourier.T

    def both_cores(main, extra, act):
        @pl.when(core == 0)
        def _():
            act(main)

        @pl.when(core == 1)
        def _():
            act(main + extra)

    def peer_copy(send, recv, ss, rs, i, count):
        to = lax.rem(me + i, WAVES)
        return pltpu.make_async_remote_copy(
            send.at[to, pl.ds(0, count)], recv.at[me, pl.ds(0, count)], ss, rs,
            device_id=(to, lev), device_id_type=MESH,
        )

    def send_all(bufs, main, extra):
        def start(count):
            @pl.loop(1, WAVES, unroll=7)
            def _(i):
                peer_copy(*bufs, i, count).start()

        both_cores(main, extra, start)
        bufs[1][me] = bufs[0][me]

    def wait_all(bufs, main, extra):
        send, recv, ss, rs = bufs

        def wait(count):
            window = (pl.ds(0, WAVES - 1), pl.ds(0, count))
            pltpu.make_async_copy(send.at[window], send.at[window], ss).wait()
            pltpu.make_async_copy(recv.at[window], recv.at[window], rs).wait()

        both_cores(main, extra, wait)

    fl = (send_fl, recv_fl, fl_ss, fl_rs)
    fh = (send_fh, recv_fh, fh_ss, fh_rs)
    bl = (send_bl, recv_bl, bl_ss, bl_rs)
    bh = (send_bh, recv_bh, bh_ss, bh_rs)

    def pack(stage, send, rows, main, extra):
        @pl.loop(0, WAVES, unroll=8)
        def _(w):
            for q in range(main):
                send[w, q] = stage[pl.ds(w * rows + TILE * q, TILE), :].astype(BF16)

        @pl.when(core == 1)
        def _():
            @pl.loop(0, WAVES // 2, unroll=8)
            def _(e):
                base = (WAVES + e) * rows
                for q in range(extra):
                    first = stage[pl.ds(base + TILE * q, TILE), :]
                    second = stage[pl.ds(base + rows // 2 + TILE * q, TILE), :]
                    second = pltpu.roll(second, 64, 1)
                    send[2 * e, main + q] = jnp.where(lane4 < 64, first, second).astype(BF16)
                    send[2 * e + 1, main + q] = jnp.where(lane4 < 64, second, first).astype(BF16)

    recurrence_phase0 = recurrence_phase(0, cosine, state, alpha_ref, both_ref, tabs)
    pass_on(light_groups)
    state = recurrence_phase(1, cosine, recurrence_phase0, alpha_ref, both_ref, tabs)
    pass_last(light_groups)
    pass_on(heavy_groups)
    own_copy().wait()
    gathered(light_groups)

    for r in range(HEAVY, ROWS):
        legendre_row(r)
    pack(stage_l, send_fl, LIGHT, 3, 2)
    send_all(fl, 3, 2)

    recurrence_phase(2, cosine, state, alpha_ref, both_ref, tabs)
    pass_last(heavy_groups)
    gathered(heavy_groups)
    for r in range(HEAVY):
        legendre_row(r)
    pack(stage_h, send_fh, HEAVY, 2, 1)
    send_all(fh, 2, 1)

    fields = pick_fields()

    def unpack(recv, rows, main, extra):
        @pl.loop(0, WAVES, unroll=8)
        def _(d):
            base = d * rows
            for q in range(main):
                flat0[pl.ds(base + TILE * q, TILE), :] = recv[d, q].astype(F32)

        @pl.when(core == 1)
        def _():
            odd = me % 2 == 1

            @pl.loop(0, WAVES, unroll=8)
            def _(d):
                base = d * rows
                later = []
                for q in reversed(range(extra)):
                    here = recv[d, main + q].astype(F32)
                    there = pltpu.roll(here, 64, 1)
                    flat1[pl.ds(base + TILE * q, TILE), :] = jnp.where(odd, there, here)
                    later.append((base + rows // 2 + TILE * q, jnp.where(odd, here, there)))
                for place, value in reversed(later):
                    flat1[pl.ds(place, TILE), :] = value

    def build(first_row, count):
        @pl.loop(0, count // LANES)
        def _(b):
            local = pl.ds(pl.multiple_of(b * LANES, LANES), LANES)
            rows = pl.ds(pl.multiple_of(first_row + b * LANES, LANES), LANES)
            raw = jnp.concatenate([flat0[local, :], flat1[local, :]], axis=1).astype(BF16)
            picked = jnp.dot(raw, fields, preferred_element_type=F32)
            even = even_ref[rows, :]
            even = jnp.concatenate([even, even], axis=1)
            for part, ref in ((0, x_re), (1, x_im)):
                both = picked[:, 256 * part : 256 * part + 256]
                evens = both * even
                ref[rows, :] = jnp.concatenate([evens, both - evens], axis=1).astype(BF16)

    light = pl.ds(0, LIGHT_COLS)
    heavy = pl.ds(LIGHT_COLS, COLS - LIGHT_COLS)

    wait_all(fl, 3, 2)
    unpack(recv_fl, LIGHT, 3, 2)
    build(0, LIGHT_COLS)

    @pl.loop(0, XROWS // XBLK)
    def _(b):
        rows = pl.ds(pl.multiple_of(b * XBLK, 16), XBLK)
        acc_c[rows, :] = jnp.dot(cos_xj[rows, light], x_re[light, :], preferred_element_type=F32)
        acc_s[rows, :] = jnp.dot(sin_xj[rows, light], x_im[light, :], preferred_element_type=F32)

    wait_all(fh, 2, 1)
    unpack(recv_fh, HEAVY, 2, 1)
    build(LIGHT_COLS, COLS - LIGHT_COLS)

    @pl.loop(0, XROWS // XBLK)
    def _(b):
        rows = pl.ds(pl.multiple_of(b * XBLK, 16), XBLK)
        c = acc_c[rows, :] + jnp.dot(
            cos_xj[rows, heavy], x_re[heavy, :], preferred_element_type=F32
        )
        s = acc_s[rows, :] + jnp.dot(
            sin_xj[rows, heavy], x_im[heavy, :], preferred_element_type=F32
        )
        c_sum, c_dif = c[:, :256] + c[:, 256:], c[:, :256] - c[:, 256:]
        s_sum, s_dif = s[:, :256] + s[:, 256:], s[:, :256] - s[:, 256:]

        def flux(g):
            return g[:, :128] * g[:, 128:]

        x = iota((XBLK, LANES), 0) + b * XBLK
        once = jnp.where((x == 0) | (x == LON // 4), 0.5, 1.0)
        f1 = flux(c_sum - s_sum) * once
        f2 = flux(c_sum + s_sum) * once
        f3 = flux(c_dif + s_dif) * once
        f4 = flux(c_dif - s_dif) * once
        near, far = f1 + f2, f3 + f4
        near_d, far_d = f2 - f1, f3 - f4
        h_c[rows, :] = jnp.concatenate([near + far, near - far], axis=1).astype(BF16)
        h_s[rows, :] = jnp.concatenate([near_d + far_d, near_d - far_d], axis=1).astype(BF16)

    places = place_fluxes()

    def direct(first_row, count):
        @pl.loop(0, count // LANES)
        def _(b):
            local = pl.ds(pl.multiple_of(b * LANES, LANES), LANES)
            rows = pl.ds(pl.multiple_of(first_row + b * LANES, LANES), LANES)
            c = jnp.dot(cos_jx[rows, :], h_c[...], preferred_element_type=F32)
            s = jnp.dot(sin_jx[rows, :], h_s[...], preferred_element_type=F32)
            even = even_ref[rows, :] > 0.5
            c = jnp.where(even, c[:, :128], c[:, 128:])
            s = jnp.where(even, s[:, :128], s[:, 128:])
            back = jnp.dot(
                jnp.concatenate([c, s], axis=1).astype(BF16), places, preferred_element_type=F32
            )
            flat0[local, :] = back[:, :LANES]
            flat1[local, :] = back[:, LANES:]

    def pack_back(send, rows, main, extra):
        @pl.loop(0, WAVES, unroll=8)
        def _(d):
            base = d * rows
            for q in range(main):
                send[d, q] = flat0[pl.ds(base + TILE * q, TILE), :].astype(BF16)

        @pl.when(core == 1)
        def _():
            @pl.loop(0, WAVES, unroll=8)
            def _(d):
                base = d * rows
                for q in range(extra):
                    first = flat1[pl.ds(base + TILE * q, TILE), :]
                    second = flat1[pl.ds(base + rows // 2 + TILE * q, TILE), :]
                    send[d, main + q] = jnp.where(lane4 < 64, first, second).astype(BF16)

    direct(LIGHT_COLS, COLS - LIGHT_COLS)
    pack_back(send_bh, HEAVY, 2, 1)
    send_all(bh, 2, 1)
    direct(0, LIGHT_COLS)
    pack_back(send_bl, LIGHT, 3, 2)
    send_all(bl, 3, 2)

    def unpack_back(recv, stage, rows, main, extra):
        @pl.loop(0, WAVES, unroll=8)
        def _(w):
            for q in range(main):
                stage[pl.ds(w * rows + TILE * q, TILE), :] = recv[w, q].astype(F32)

        @pl.when(core == 1)
        def _():
            @pl.loop(0, WAVES // 2, unroll=8)
            def _(e):
                base = (WAVES + e) * rows
                later = []
                for q in reversed(range(extra)):
                    low = recv[2 * e, main + q].astype(F32)
                    high = recv[2 * e + 1, main + q].astype(F32)
                    first = jnp.where(lane4 < 64, low, pltpu.roll(high, 64, 1))
                    second = jnp.where(lane4 < 64, pltpu.roll(low, 64, 1), high)
                    stage[pl.ds(base + TILE * q, TILE), :] = first
                    later.append((base + rows // 2 + TILE * q, second))
                for place, value in reversed(later):
                    stage[pl.ds(place, TILE), :] = value

    def e1_copy(g):
        window = (slice(None), pl.ds(2 * g, 2), slice(None), pl.ds(0, WIDTHS[g]))
        return pltpu.make_async_remote_copy(
            partial.at[(1 - core,) + window], e1_recv.at[window], e1_ss.at[g], e1_rs.at[g],
            device_id=(me, partner), device_id_type=MESH,
        )

    def row_piece(ref, g):
        return ref.at[pl.ds(2 * g, 2), :, pl.ds(0, WIDTHS[g])]

    def ends(g):
        near, far = lax.rem(y + 1, 4), lax.rem(y + 3, 4)
        return (near, up, far, down) if g in UP else (far, down, near, up)

    def rel_copy(g):
        return pltpu.make_async_remote_copy(
            piece(e2_send, lax.rem(y + 2, 4), g), row_piece(rel_recv, g), rel_ss.at[g], rel_rs.at[g],
            device_id=(me, ends(g)[1]), device_id_type=MESH,
        )

    def e2_copy(g):
        return pltpu.make_async_remote_copy(
            piece(e2_send, ends(g)[2], g), piece(e2_recv, 1, g), e2_ss.at[g], e2_rs.at[g],
            device_id=(me, ends(g)[3]), device_id_type=MESH,
        )

    def sum_copy(g):
        return pltpu.make_async_remote_copy(
            row_piece(e2_sum, g), piece(e2_recv, 0, g), sum_ss.at[g], sum_rs.at[g],
            device_id=(me, ends(g)[1]), device_id_type=MESH,
        )

    def add_cores(g):
        e1_copy(g).wait()
        for r in (2 * g, 2 * g + 1):
            for q in range(4):
                mine = partial[core, q, r, :, 0 : WIDTHS[g]].astype(F32)
                other = e1_recv[q, r, :, 0 : WIDTHS[g]].astype(F32)
                e2_send[q, r, :, 0 : WIDTHS[g]] = (mine + other).astype(BF16)
        rel_copy(g).start()
        e2_copy(g).start()

    def add_relayed(g):
        rel_copy(g).wait()
        for r in (2 * g, 2 * g + 1):
            mine = e2_send[ends(g)[0], r, :, 0 : WIDTHS[g]].astype(F32)
            other = rel_recv[r, :, 0 : WIDTHS[g]].astype(F32)
            e2_sum[r, :, 0 : WIDTHS[g]] = (mine + other).astype(BF16)
        sum_copy(g).start()

    def flux_rows(g):
        width = WIDTHS[g]
        for r in (2 * g, 2 * g + 1):
            table = table_rows(tabs, r, width)
            order = wo_ref[me * ROWS + r]
            weight = jnp.where(order == 0, 1.0, 0.5)
            factor = jnp.where(order < cut, area * weight, 0.0)
            if r < HEAVY:
                back = stage_h[pl.ds(r, LANES, stride=HEAVY), :]
            else:
                back = stage_l[pl.ds(r - HEAVY, LANES, stride=LIGHT), :]
            sums = lax.dot_general(
                (back.T * factor).astype(BF16), table, (((1,), (1,)), ((), ())),
                preferred_element_type=F32,
            )
            sums = sums.reshape(LEVS, 2, 8, width)
            sums = (sums[:, 0] + sums[:, 1] * sign[:, :width]).astype(BF16)
            for l in range(LEVS):
                partial[l % 2, l // 2, r, :, 0:width] = sums[l]
        e1_copy(g).start()

    wait_all(bh, 2, 1)
    unpack_back(recv_bh, stage_h, HEAVY, 2, 1)
    for g in range(GROUPS):
        if g == HEAVY // 2:
            add_cores(g - 1)
            add_relayed(g - 2)
            add_relayed(g - 1)
            wait_all(bl, 3, 2)
            unpack_back(recv_bl, stage_l, LIGHT, 3, 2)
        flux_rows(g)
        if g > 0 and g != HEAVY // 2:
            add_cores(g - 1)
        if g > 1 and g not in (HEAVY // 2, HEAVY // 2 + 1):
            add_relayed(g - 2)
    add_cores(GROUPS - 1)
    add_relayed(GROUPS - 2)
    add_relayed(GROUPS - 1)
    for g in range(GROUPS):
        width = WIDTHS[g]
        e2_copy(g).wait()
        sum_copy(g).wait()
        for r in (2 * g, 2 * g + 1):
            total = e2_send[y, r, :, 0:width].astype(F32) + e2_recv[0, r, :, 0:width].astype(F32)
            total = total + e2_recv[1, r, :, 0:width].astype(F32)
            out_ref[0, r, :, 0:width] = total.astype(BF16)
            if width < TOP:
                out_ref[0, r, :, width:TOP] = jnp.zeros((8, TOP - width), BF16)


def on_device(spectra, wave_order, truncation):
    by_peer = wave_order.reshape(WAVES, ROWS)
    orders = jnp.concatenate(
        [by_peer[:, HEAVY:].reshape(LIGHT_COLS), by_peer[:, :HEAVY].reshape(COLS - LIGHT_COLS), truncation]
    ).reshape(2 * COLS // LANES, LANES)
    vmem = pl.BlockSpec(memory_space=pltpu.VMEM)
    dma = pltpu.SemaphoreType.DMA
    message = lambda tiles: pltpu.VMEM((WAVES, tiles, TILE, LANES), BF16)
    flux = pl.pallas_call(
        kernel,
        out_shape=jax.ShapeDtypeStruct((1, ROWS, 8, TOP), BF16),
        in_specs=[pl.BlockSpec(memory_space=pltpu.SMEM), vmem, pl.BlockSpec(memory_space=pl.ANY)],
        out_specs=vmem,
        scratch_shapes=[
            pltpu.VMEM((10, ROWS_PAD, LANES), F32),
            pltpu.VMEM((10, ROWS_PAD, LANES), F32),
            pltpu.VMEM((8 * TAB_STRIDE[0], LANES), F32),
            pltpu.VMEM((8 * TAB_STRIDE[1], LANES), F32),
            pltpu.VMEM((8 * TAB_STRIDE[2], LANES), F32),
            pltpu.VMEM((XPAD, COLS), BF16),
            pltpu.VMEM((XPAD, COLS), BF16),
            pltpu.VMEM((COLS, XPAD), BF16),
            pltpu.VMEM((COLS, XPAD), BF16),
            pltpu.VMEM((COLS, LANES), F32),
            pltpu.VMEM((LEVS, ROWS, 8, TOP), BF16),
            pltpu.VMEM((LANES * LIGHT + 8, LANES), F32),
            pltpu.VMEM((LANES * HEAVY + 8, LANES), F32),
            message(5), message(3), message(5), message(3),
            message(5), message(3), message(5), message(3),
            pltpu.VMEM((LIGHT_COLS + 8, LANES), F32),
            pltpu.VMEM((LIGHT_COLS + 8, LANES), F32),
            pltpu.VMEM((COLS, 512), BF16),
            pltpu.VMEM((COLS, 512), BF16),
            pltpu.VMEM((XROWS, 512), F32),
            pltpu.VMEM((XROWS, 512), F32),
            pltpu.VMEM((XPAD, 256), BF16),
            pltpu.VMEM((XPAD, 256), BF16),
            pltpu.VMEM((2, 4, ROWS, 8, TOP), BF16),
            pltpu.VMEM((4, ROWS, 8, TOP), BF16),
            pltpu.VMEM((4, ROWS, 8, TOP), BF16),
            pltpu.VMEM((ROWS, 8, TOP), BF16),
            pltpu.VMEM((ROWS, 8, TOP), BF16),
            pltpu.VMEM((2, ROWS, 8, TOP), BF16),
            dma,
            dma((2, GROUPS)), dma((2, GROUPS)), dma((GROUPS,)), dma((GROUPS,)),
            dma((4, GROUPS)), dma((4, GROUPS)),
            dma, dma, dma, dma, dma, dma, dma, dma,
            dma((GROUPS,)), dma((GROUPS,)), dma((GROUPS,)), dma((GROUPS,)),
            dma((GROUPS,)), dma((GROUPS,)), dma((GROUPS,)), dma((GROUPS,)),
        ],
        compiler_params=pltpu.CompilerParams(
            collective_id=0, has_side_effects=True, vmem_limit_bytes=60 * 2**20
        ),
        name="flux_transform",
    )(wave_order, orders, spectra)
    return flux.astype(F32)


def solution(mesh):
    return jax.shard_map(
        on_device,
        mesh=mesh,
        in_specs=(P("lev", "wave", None, None), P(), P()),
        out_specs=P("lev", "wave", None, None),
        check_vma=False,
    )
```

time: 123 us -> 105 us (0.85)
  Pallas kernels: 119 us -> 99.5 us
  other arithmetic: 0 us -> 2.55 us
  local copies, waits for them, and re-layouts: 3.57 us -> 1.65 us
    pallas_call x1, Pallas kernels: 119 us -> 99.5 us  [on_device(): pl.pallas_call(kernel, out_shape=jax.ShapeDtypeStruct((1, ROWS, 8, TOP),...]
    convert_element_type x0 -> x1, other arithmetic: none -> 1.95 us  [on_device(): return flux.astype(F32)]
    unnamed x1 -> x2, local copies, waits for them, and re-layouts: 2.09 us -> 0.59 us
where the time goes in v2:
time: 105 us; the launch traced here: 104 us
  Pallas kernels  99.5 us (95%)
  other arithmetic  2.55 us (2%)
  local copies, waits for them, and re-layouts  1.65 us (2%)
    pallas_call x1, Pallas kernels, on_device(): pl.pallas_call(kernel, out_shape=jax.ShapeDtypeStruct((1, ROWS, 8, TOP),...  99.5 us

profile of v2, /device:TPU:1, one launch (start us, length us, event | category | flops | bytes accessed | tf_op | source)
XLA Modules:
  0.0 103.7 jit_solution(5765186481291797401)
XLA Ops:
  0.0 0.8 reshape.12
  0.8 0.1 reshape.14
  0.9 0.1 slice.8
  1.0 0.0 copy-start
  1.0 0.1 reshape.13
  1.1 0.6 copy-done
  1.7 0.6 add_bitcast_fusion.mt_ref
  2.3 99.5 %flux_transform.1 = bf16[1,20,8,1280]{3,2,1,0:T(8,128)(2,1)} custom-call(s32[1280]{0:T(1024)} %wo_ref.1, s32[20,128]{1,0:T(8,128)} %add_bitcast_fusion.mt_ref, bf16[1,20,8,1280]{3,2,1,0:T(8,128)(2,1)} %spec_ref.1), custom_call_target="tpu_custom_call" | custom-call | tf_op jit(solution)/shard_map/flux_transform/pallas_call | solution.py:657
  101.7 1.9 %convert_element_type.3 = f32[1,20,8,1280]{3,2,1,0:T(8,128)} convert(bf16[1,20,8,1280]{3,2,1,0:T(8,128)(2,1)} %flux_transform.1) | non-fusion elementwise | flops 204800 | bytes 1228800 | tf_op jit(solution)/shard_map/convert_element_type | solution.py:704
Async XLA Ops:
  1.0 0.7 copy-start

commit v3 on v2

--- a/solution.py
+++ b/solution.py
@@ -32,7 +32,6 @@
 XPAD = 768
 XBLK = 112
 TILE = 4
-UP = (0, 3, 4, 7, 8)
 
 
 def iota(shape, dim):
@@ -205,29 +204,35 @@
     cos_xj, sin_xj, cos_jx, sin_jx, even_ref,
     gath, stage_l, stage_h, send_fl, send_fh, recv_fl, recv_fh, send_bl, send_bh, recv_bl, recv_bh,
     flat0, flat1, x_re, x_im, acc_c, acc_s, h_c, h_s,
-    partial, e1_recv, e2_send, e2_sum, rel_recv, e2_recv,
-    own_sem, g_send, g_recv, r_send, r_recv, c_send, c_recv,
+    partial, e1_recv, e2_send, e2_recv,
+    z_ready, own_sem, g_send, g_recv, c_send, c_recv,
     fl_ss, fl_rs, fh_ss, fh_rs, bl_ss, bl_rs, bh_ss, bh_rs,
-    e1_ss, e1_rs, rel_ss, rel_rs, e2_ss, e2_rs, sum_ss, sum_rs,
+    e1_ss, e1_rs, e2_ss, e2_rs,
 ):
     me = lax.axis_index("wave")
     lev = lax.axis_index("lev")
     y = lev // 2
     core = lev % 2
     partner = y * 2 + (1 - core)
-    up = lax.rem(lev + 2, LEVS)
-    down = lax.rem(lev + 6, LEVS)
+    x = lax.rem(me, 4)
     tabs = (tab0, tab1, tab2)
     lane4 = iota((TILE, LANES), 1)
 
     barrier = pltpu.get_barrier_semaphore()
-    for other in (up, down, partner):
-        pl.semaphore_signal(barrier, inc=1, device_id=(me, other), device_id_type=MESH)
-
-    @pl.loop(1, WAVES)
-    def _(i):
+    for i in range(1, 4):
         pl.semaphore_signal(
-            barrier, inc=1, device_id=(lax.rem(me + i, WAVES), lev), device_id_type=MESH
+            barrier, inc=1, device_id=(me, lax.rem(lev + 2 * i, LEVS)), device_id_type=MESH
+        )
+    pl.semaphore_signal(barrier, inc=1, device_id=(me, partner), device_id_type=MESH)
+
+    def x_peer(i):
+        return me - x + lax.rem(x + i, 4)
+
+    for i in range(1, 4):
+        pl.semaphore_signal(barrier, inc=1, device_id=(x_peer(i), lev), device_id_type=MESH)
+    for i in range(1, WAVES // 4):
+        pl.semaphore_signal(
+            barrier, inc=1, device_id=(lax.rem(me + 4 * i, WAVES), lev), device_id_type=MESH
         )
 
     lat0 = first_latitude(lev)
@@ -238,8 +243,9 @@
     h_c[pl.ds(XROWS, XPAD - XROWS), :] = jnp.zeros((XPAD - XROWS, 256), BF16)
     h_s[pl.ds(XROWS, XPAD - XROWS), :] = jnp.zeros((XPAD - XROWS, 256), BF16)
 
-    longitude_tables(mt_ref, cos_xj, sin_xj, cos_jx, sin_jx, even_ref)
-    pl.semaphore_wait(barrier, WAVES - 1 + 3)
+    pl.semaphore_wait(barrier, 3 + 1 + 3 + WAVES // 4 - 1)
+    for i in range(1, 4):
+        pl.semaphore_signal(z_ready, inc=1, device_id=(x_peer(i), lev), device_id_type=MESH)
 
     light_groups = tuple(range(HEAVY // 2, GROUPS))
     heavy_groups = tuple(range(HEAVY // 2))
@@ -250,21 +256,14 @@
     def own_copy():
         return pltpu.make_async_copy(spec_ref.at[0], gath.at[lev], own_sem)
 
-    def y_copy(way, g):
+    def y_copy(i, g):
         return pltpu.make_async_remote_copy(
-            piece(spec_ref, 0, g), piece(gath, lev, g), g_send.at[way, g], g_recv.at[way, g],
-            device_id=(me, up if way == 0 else down), device_id_type=MESH,
-        )
-
-    def relay_copy(g):
-        level = down if g in UP else up
-        return pltpu.make_async_remote_copy(
-            piece(gath, level, g), piece(gath, level, g), r_send.at[g], r_recv.at[g],
-            device_id=(me, up if g in UP else down), device_id_type=MESH,
+            piece(spec_ref, 0, g), piece(gath, lev, g), g_send.at[i, g], g_recv.at[i, g],
+            device_id=(me, lax.rem(lev + 2 * i, LEVS)), device_id_type=MESH,
         )
 
     def core_copy(i, g):
-        level = (lev, down, up, lax.rem(lev + 4, LEVS))[i]
+        level = lax.rem(lev + LEVS - 2 * i, LEVS)
         src = piece(spec_ref, 0, g) if i == 0 else piece(gath, level, g)
         return pltpu.make_async_remote_copy(
             src, piece(gath, level, g), c_send.at[i, g], c_recv.at[i, g],
@@ -273,28 +272,22 @@
 
     def pass_on(groups):
         for g in groups:
-            for way in range(2):
-                y_copy(way, g).wait()
-            relay_copy(g).start()
-            for i in (1, 2):
+            for i in range(1, 4):
+                y_copy(i, g).wait()
                 core_copy(i, g).start()
-
-    def pass_last(groups):
-        for g in groups:
-            relay_copy(g).wait()
-            core_copy(3, g).start()
 
     def gathered(groups):
         for g in groups:
             for i in range(4):
                 core_copy(i, g).wait()
 
-    for g in light_groups + heavy_groups:
-        for way in range(2):
-            y_copy(way, g).start()
+    for groups in (light_groups, heavy_groups):
+        for g in groups:
+            for i in range(1, 4):
+                y_copy(i, g).start()
+        for g in groups:
+            core_copy(0, g).start()
     own_copy().start()
-    for g in light_groups + heavy_groups:
-        core_copy(0, g).start()
 
     angles = half_angles(lat0)[0:1]
     unit = lat0 // 32
@@ -379,26 +372,26 @@
                     send[2 * e, main + q] = jnp.where(lane4 < 64, first, second).astype(BF16)
                     send[2 * e + 1, main + q] = jnp.where(lane4 < 64, second, first).astype(BF16)
 
-    recurrence_phase0 = recurrence_phase(0, cosine, state, alpha_ref, both_ref, tabs)
+    state = recurrence_phase(0, cosine, state, alpha_ref, both_ref, tabs)
+    state = recurrence_phase(1, cosine, state, alpha_ref, both_ref, tabs)
     pass_on(light_groups)
-    state = recurrence_phase(1, cosine, recurrence_phase0, alpha_ref, both_ref, tabs)
-    pass_last(light_groups)
-    pass_on(heavy_groups)
+    recurrence_phase(2, cosine, state, alpha_ref, both_ref, tabs)
     own_copy().wait()
     gathered(light_groups)
-
     for r in range(HEAVY, ROWS):
         legendre_row(r)
     pack(stage_l, send_fl, LIGHT, 3, 2)
+    pl.semaphore_wait(z_ready, 3)
     send_all(fl, 3, 2)
 
-    recurrence_phase(2, cosine, state, alpha_ref, both_ref, tabs)
-    pass_last(heavy_groups)
+    pass_on(heavy_groups)
     gathered(heavy_groups)
     for r in range(HEAVY):
         legendre_row(r)
     pack(stage_h, send_fh, HEAVY, 2, 1)
     send_all(fh, 2, 1)
+
+    longitude_tables(mt_ref, cos_xj, sin_xj, cos_jx, sin_jx, even_ref)
 
     fields = pick_fields()
 
@@ -471,8 +464,8 @@
         def flux(g):
             return g[:, :128] * g[:, 128:]
 
-        x = iota((XBLK, LANES), 0) + b * XBLK
-        once = jnp.where((x == 0) | (x == LON // 4), 0.5, 1.0)
+        place = iota((XBLK, LANES), 0) + b * XBLK
+        once = jnp.where((place == 0) | (place == LON // 4), 0.5, 1.0)
         f1 = flux(c_sum - s_sum) * once
         f2 = flux(c_sum + s_sum) * once
         f3 = flux(c_dif + s_dif) * once
@@ -553,29 +546,11 @@
             device_id=(me, partner), device_id_type=MESH,
         )
 
-    def row_piece(ref, g):
-        return ref.at[pl.ds(2 * g, 2), :, pl.ds(0, WIDTHS[g])]
-
-    def ends(g):
-        near, far = lax.rem(y + 1, 4), lax.rem(y + 3, 4)
-        return (near, up, far, down) if g in UP else (far, down, near, up)
-
-    def rel_copy(g):
+    def e2_copy(i, g):
+        to = lax.rem(y + i, 4)
         return pltpu.make_async_remote_copy(
-            piece(e2_send, lax.rem(y + 2, 4), g), row_piece(rel_recv, g), rel_ss.at[g], rel_rs.at[g],
-            device_id=(me, ends(g)[1]), device_id_type=MESH,
-        )
-
-    def e2_copy(g):
-        return pltpu.make_async_remote_copy(
-            piece(e2_send, ends(g)[2], g), piece(e2_recv, 1, g), e2_ss.at[g], e2_rs.at[g],
-            device_id=(me, ends(g)[3]), device_id_type=MESH,
-        )
-
-    def sum_copy(g):
-        return pltpu.make_async_remote_copy(
-            row_piece(e2_sum, g), piece(e2_recv, 0, g), sum_ss.at[g], sum_rs.at[g],
-            device_id=(me, ends(g)[1]), device_id_type=MESH,
+            piece(e2_send, to, g), piece(e2_recv, i - 1, g), e2_ss.at[i, g], e2_rs.at[i, g],
+            device_id=(me, to * 2 + core), device_id_type=MESH,
         )
 
     def add_cores(g):
@@ -585,16 +560,8 @@
                 mine = partial[core, q, r, :, 0 : WIDTHS[g]].astype(F32)
                 other = e1_recv[q, r, :, 0 : WIDTHS[g]].astype(F32)
                 e2_send[q, r, :, 0 : WIDTHS[g]] = (mine + other).astype(BF16)
-        rel_copy(g).start()
-        e2_copy(g).start()
-
-    def add_relayed(g):
-        rel_copy(g).wait()
-        for r in (2 * g, 2 * g + 1):
-            mine = e2_send[ends(g)[0], r, :, 0 : WIDTHS[g]].astype(F32)
-            other = rel_recv[r, :, 0 : WIDTHS[g]].astype(F32)
-            e2_sum[r, :, 0 : WIDTHS[g]] = (mine + other).astype(BF16)
-        sum_copy(g).start()
+        for i in (2, 1, 3):
+            e2_copy(i, g).start()
 
     def flux_rows(g):
         width = WIDTHS[g]
@@ -619,28 +586,24 @@
 
     wait_all(bh, 2, 1)
     unpack_back(recv_bh, stage_h, HEAVY, 2, 1)
-    for g in range(GROUPS):
-        if g == HEAVY // 2:
-            add_cores(g - 1)
-            add_relayed(g - 2)
-            add_relayed(g - 1)
-            wait_all(bl, 3, 2)
-            unpack_back(recv_bl, stage_l, LIGHT, 3, 2)
+    for g in heavy_groups:
         flux_rows(g)
-        if g > 0 and g != HEAVY // 2:
-            add_cores(g - 1)
-        if g > 1 and g not in (HEAVY // 2, HEAVY // 2 + 1):
-            add_relayed(g - 2)
-    add_cores(GROUPS - 1)
-    add_relayed(GROUPS - 2)
-    add_relayed(GROUPS - 1)
+    for g in heavy_groups:
+        add_cores(g)
+    wait_all(bl, 3, 2)
+    unpack_back(recv_bl, stage_l, LIGHT, 3, 2)
+    for g in light_groups:
+        flux_rows(g)
+    for g in light_groups:
+        add_cores(g)
     for g in range(GROUPS):
         width = WIDTHS[g]
-        e2_copy(g).wait()
-        sum_copy(g).wait()
+        for i in range(1, 4):
+            e2_copy(i, g).wait()
         for r in (2 * g, 2 * g + 1):
-            total = e2_send[y, r, :, 0:width].astype(F32) + e2_recv[0, r, :, 0:width].astype(F32)
-            total = total + e2_recv[1, r, :, 0:width].astype(F32)
+            total = e2_send[y, r, :, 0:width].astype(F32)
+            for i in range(3):
+                total = total + e2_recv[i, r, :, 0:width].astype(F32)
             out_ref[0, r, :, 0:width] = total.astype(BF16)
             if width < TOP:
                 out_ref[0, r, :, width:TOP] = jnp.zeros((8, TOP - width), BF16)
@@ -686,15 +649,12 @@
             pltpu.VMEM((2, 4, ROWS, 8, TOP), BF16),
             pltpu.VMEM((4, ROWS, 8, TOP), BF16),
             pltpu.VMEM((4, ROWS, 8, TOP), BF16),
-            pltpu.VMEM((ROWS, 8, TOP), BF16),
-            pltpu.VMEM((ROWS, 8, TOP), BF16),
-            pltpu.VMEM((2, ROWS, 8, TOP), BF16),
+            pltpu.VMEM((3, ROWS, 8, TOP), BF16),
+            pltpu.SemaphoreType.REGULAR,
             dma,
-            dma((2, GROUPS)), dma((2, GROUPS)), dma((GROUPS,)), dma((GROUPS,)),
-            dma((4, GROUPS)), dma((4, GROUPS)),
+            dma((4, GROUPS)), dma((4, GROUPS)), dma((4, GROUPS)), dma((4, GROUPS)),
             dma, dma, dma, dma, dma, dma, dma, dma,
-            dma((GROUPS,)), dma((GROUPS,)), dma((GROUPS,)), dma((GROUPS,)),
-            dma((GROUPS,)), dma((GROUPS,)), dma((GROUPS,)), dma((GROUPS,)),
+            dma((GROUPS,)), dma((GROUPS,)), dma((4, GROUPS)), dma((4, GROUPS)),
         ],
         compiler_params=pltpu.CompilerParams(
             collective_id=0, has_side_effects=True, vmem_limit_bytes=60 * 2**20

time: 105 us -> 93.7 us (0.89)
  Pallas kernels: 99.5 us -> 89.1 us
    pallas_call x1, Pallas kernels: 99.5 us -> 89.1 us  [on_device(): pl.pallas_call(kernel, out_shape=jax.ShapeDtypeStruct((1, ROWS, 8, TOP),...]
where the time goes in v3:
time: 93.7 us; the launch traced here: 93.4 us
  Pallas kernels  89.1 us (95%)
  other arithmetic  2.55 us (3%)
  local copies, waits for them, and re-layouts  1.65 us (2%)
    pallas_call x1, Pallas kernels, on_device(): pl.pallas_call(kernel, out_shape=jax.ShapeDtypeStruct((1, ROWS, 8, TOP),...  89.1 us
    convert_element_type x1, other arithmetic, on_device(): return flux.astype(F32)  1.95 us

profile of v3, /device:TPU:1, one launch (start us, length us, event | category | flops | bytes accessed | tf_op | source)
XLA Modules:
  0.0 93.4 jit_solution(7502135152220614782)
XLA Ops:
  0.0 0.8 reshape.12
  0.8 0.1 reshape.14
  0.9 0.1 slice.8
  1.0 0.0 copy-start
  1.0 0.1 reshape.13
  1.1 0.6 copy-done
  1.7 0.6 add_bitcast_fusion.mt_ref
  2.3 89.1 %flux_transform.1 = bf16[1,20,8,1280]{3,2,1,0:T(8,128)(2,1)} custom-call(s32[1280]{0:T(1024)} %wo_ref.1, s32[20,128]{1,0:T(8,128)} %add_bitcast_fusion.mt_ref, bf16[1,20,8,1280]{3,2,1,0:T(8,128)(2,1)} %spec_ref.1), custom_call_target="tpu_custom_call" | custom-call | tf_op jit(solution)/shard_map/flux_transform/pallas_call | solution.py:620
  91.4 1.9 %convert_element_type.3 = f32[1,20,8,1280]{3,2,1,0:T(8,128)} convert(bf16[1,20,8,1280]{3,2,1,0:T(8,128)(2,1)} %flux_transform.1) | non-fusion elementwise | flops 204800 | bytes 1228800 | tf_op jit(solution)/shard_map/convert_element_type | solution.py:664
Async XLA Ops:
  1.0 0.7 copy-start

commit v4 on v3

--- a/solution.py
+++ b/solution.py
@@ -16,7 +16,6 @@
 LON = 2560
 ROWS = 20
 ROWS_PAD = 24
-LIGHT = 12
 HEAVY = 8
 WAVES = 64
 LEVS = 8
@@ -27,11 +26,16 @@
 TAB_LEN = (1280, 768, 256)
 TAB_STRIDE = (1288, 776, 264)
 COLS = WAVES * ROWS
-LIGHT_COLS = WAVES * LIGHT
+HEAVY_COLS = WAVES * HEAVY
 XROWS = 672
 XPAD = 768
-XBLK = 112
+XBLK = 224
 TILE = 4
+HEAVY_TILES = (0, 1)
+LIGHT_TILES = (2, 3, 4)
+HEAVY_PAIRS = ((0, 1),)
+LIGHT_PAIRS = ((2, 3), (4, 4))
+HALF = WAVES // 2
 
 
 def iota(shape, dim):
@@ -136,6 +140,29 @@
     sine = jnp.where((quarter == 2.0) | (quarter == 3.0), -sine, sine)
     cosine = jnp.where((quarter == 1.0) | (quarter == 2.0), -cosine, cosine)
     return sine, cosine
+
+
+def flat_row(tile, half):
+    if tile < 2:
+        return (2 * half + tile) * LANES
+    return (4 + 3 * half + tile - 2) * LANES
+
+
+def column_orders(wo_ref, z, mt_ref):
+    lane = iota((8, LANES), 1)
+
+    @pl.loop(0, COLS // LANES)
+    def _(jb):
+        half = jnp.where(jb < 4, jb // 2, (jb - 4) // 3)
+        tile = jnp.where(jb < 4, jb % 2, 2 + (jb - 4) % 3)
+        orders = jnp.zeros((8, LANES), jnp.int32)
+        for n in range(8):
+            plane = lax.rem(z + 4 + 8 * half + n, 16)
+            base = plane * (4 * ROWS) + tile * TILE
+            for k in range(16):
+                value = wo_ref[base + (k // TILE) * ROWS + k % TILE]
+                orders = jnp.where(lane == 16 * n + k, value, orders)
+        mt_ref[pl.ds(jb, 1), :] = orders[0:1]
 
 
 def longitude_tables(mt_ref, cos_xj, sin_xj, cos_jx, sin_jx, even_ref):
@@ -199,13 +226,14 @@
 
 
 def kernel(
-    wo_ref, mt_ref, spec_ref, out_ref,
+    wo_hbm, trunc_hbm, spec_ref, out_ref,
+    wo_ref, trunc_ref, mt_ref,
     alpha_ref, both_ref, tab0, tab1, tab2,
     cos_xj, sin_xj, cos_jx, sin_jx, even_ref,
-    gath, stage_l, stage_h, send_fl, send_fh, recv_fl, recv_fh, send_bl, send_bh, recv_bl, recv_bh,
+    gath, stage, send_fl, send_fh, recv_fl, recv_fh, send_bl, send_bh, recv_bl, recv_bh,
     flat0, flat1, x_re, x_im, acc_c, acc_s, h_c, h_s,
     partial, e1_recv, e2_send, e2_recv,
-    z_ready, own_sem, g_send, g_recv, c_send, c_recv,
+    in_sem, ready, own_sem, g_send, g_recv, c_send, c_recv,
     fl_ss, fl_rs, fh_ss, fh_rs, bl_ss, bl_rs, bh_ss, bh_rs,
     e1_ss, e1_rs, e2_ss, e2_rs,
 ):
@@ -215,8 +243,22 @@
     core = lev % 2
     partner = y * 2 + (1 - core)
     x = lax.rem(me, 4)
+    z = me // 4
     tabs = (tab0, tab1, tab2)
     lane4 = iota((TILE, LANES), 1)
+
+    inputs = (
+        pltpu.make_async_copy(wo_hbm, wo_ref, in_sem.at[0]),
+        pltpu.make_async_copy(trunc_hbm, trunc_ref, in_sem.at[1]),
+    )
+    for copy in inputs:
+        copy.start()
+
+    def z_peer(i):
+        return lax.rem(me + 4 * i + WAVES, WAVES)
+
+    def x_peer(i):
+        return me - x + lax.rem(x + i, 4)
 
     barrier = pltpu.get_barrier_semaphore()
     for i in range(1, 4):
@@ -224,28 +266,32 @@
             barrier, inc=1, device_id=(me, lax.rem(lev + 2 * i, LEVS)), device_id_type=MESH
         )
     pl.semaphore_signal(barrier, inc=1, device_id=(me, partner), device_id_type=MESH)
-
-    def x_peer(i):
-        return me - x + lax.rem(x + i, 4)
-
-    for i in range(1, 4):
-        pl.semaphore_signal(barrier, inc=1, device_id=(x_peer(i), lev), device_id_type=MESH)
-    for i in range(1, WAVES // 4):
-        pl.semaphore_signal(
-            barrier, inc=1, device_id=(lax.rem(me + 4 * i, WAVES), lev), device_id_type=MESH
-        )
-
+    for peer in (z_peer(1), z_peer(-1), x_peer(1), x_peer(2), x_peer(3)):
+        pl.semaphore_signal(barrier, inc=1, device_id=(peer, lev), device_id_type=MESH)
+
+    def say(step):
+        reach = (1, 2, 4)
+        if step < 3:
+            peers = (z_peer(reach[step]), z_peer(-reach[step]))
+        else:
+            peers = (x_peer(1), x_peer(2), x_peer(3))
+        for peer in peers:
+            pl.semaphore_signal(ready.at[step], inc=1, device_id=(peer, lev), device_id_type=MESH)
+
+    def hear(step):
+        pl.semaphore_wait(ready.at[step], 2 if step < 3 else 3)
+
+    for copy in inputs:
+        copy.wait()
     lat0 = first_latitude(lev)
     orders = own_orders(wo_ref, me * ROWS)
     cosine, state = recurrence_start(wo_ref, me * ROWS, orders, lat0, alpha_ref, both_ref)
-    flat0[...] = jnp.zeros_like(flat0)
     flat1[...] = jnp.zeros_like(flat1)
     h_c[pl.ds(XROWS, XPAD - XROWS), :] = jnp.zeros((XPAD - XROWS, 256), BF16)
     h_s[pl.ds(XROWS, XPAD - XROWS), :] = jnp.zeros((XPAD - XROWS, 256), BF16)
 
-    pl.semaphore_wait(barrier, 3 + 1 + 3 + WAVES // 4 - 1)
-    for i in range(1, 4):
-        pl.semaphore_signal(z_ready, inc=1, device_id=(x_peer(i), lev), device_id_type=MESH)
+    pl.semaphore_wait(barrier, 9)
+    say(0)
 
     light_groups = tuple(range(HEAVY // 2, GROUPS))
     heavy_groups = tuple(range(HEAVY // 2))
@@ -290,12 +336,10 @@
     own_copy().start()
 
     angles = half_angles(lat0)[0:1]
-    unit = lat0 // 32
-    cut_row = COLS // LANES + unit // 4
-    wide = jnp.concatenate([mt_ref[pl.ds(cut_row, 1), :], mt_ref[pl.ds(cut_row + 1, 1), :]], axis=1)
-    cut = wide[:, 0:LANES]
-    for n in range(1, 4):
-        cut = jnp.where(unit % 4 == n, wide[:, 32 * n : 32 * n + LANES], cut)
+    lane = iota((1, LANES), 1)
+    cut = jnp.zeros((1, LANES), jnp.int32)
+    for n in range(LANES):
+        cut = jnp.where(lane == n, trunc_ref[lat0 + n], cut)
     area = (float(TOP) / LON) * (math.pi / TOP) * jnp.sin(angles)
     area = jnp.where(iota((1, LANES), 1) < 64 + 32 * core, area, 0.0)
     sign = jnp.where(iota((1, TOP), 1) % 2 == 0, 1.0, -1.0)
@@ -309,10 +353,7 @@
         order = wo_ref[me * ROWS + r]
         weight = jnp.where(order == 0, 1.0, 2.0)
         fourier = fourier * jnp.where(order < cut, weight, 0.0)
-        if r < HEAVY:
-            stage_h[pl.ds(r, LANES, stride=HEAVY), :] = fourier.T
-        else:
-            stage_l[pl.ds(r - HEAVY, LANES, stride=LIGHT), :] = fourier.T
+        stage[pl.ds(r // TILE * 512 + r % TILE, LANES, stride=TILE), :] = fourier.T
 
     def both_cores(main, extra, act):
         @pl.when(core == 0)
@@ -323,21 +364,27 @@
         def _():
             act(main + extra)
 
-    def peer_copy(send, recv, ss, rs, i, count):
-        to = lax.rem(me + i, WAVES)
-        return pltpu.make_async_remote_copy(
-            send.at[to, pl.ds(0, count)], recv.at[me, pl.ds(0, count)], ss, rs,
-            device_id=(to, lev), device_id_type=MESH,
-        )
-
-    def send_all(bufs, main, extra):
+    def peer(half, t):
+        return lax.rem(z + 4 + 8 * half + t // 4, 16) * 4 + lax.rem(t, 4)
+
+    def send_half(bufs, half, main, extra):
+        send, recv, ss, rs = bufs
+
         def start(count):
-            @pl.loop(1, WAVES, unroll=7)
-            def _(i):
-                peer_copy(*bufs, i, count).start()
+            @pl.loop(0, HALF, unroll=4)
+            def _(t):
+                to = peer(half, t)
+
+                @pl.when(to != me)
+                def _():
+                    pltpu.make_async_remote_copy(
+                        send.at[to, pl.ds(0, count)], recv.at[me, pl.ds(0, count)], ss, rs,
+                        device_id=(to, lev), device_id_type=MESH,
+                    ).start()
 
         both_cores(main, extra, start)
-        bufs[1][me] = bufs[0][me]
+        if half == 1:
+            recv[me] = send[me]
 
     def wait_all(bufs, main, extra):
         send, recv, ss, rs = bufs
@@ -354,76 +401,84 @@
     bl = (send_bl, recv_bl, bl_ss, bl_rs)
     bh = (send_bh, recv_bh, bh_ss, bh_rs)
 
-    def pack(stage, send, rows, main, extra):
+    def pack(send, tiles, pairs):
         @pl.loop(0, WAVES, unroll=8)
         def _(w):
-            for q in range(main):
-                send[w, q] = stage[pl.ds(w * rows + TILE * q, TILE), :].astype(BF16)
+            for q, tile in enumerate(tiles):
+                send[w, q] = stage[pl.ds(tile * 512 + TILE * w, TILE), :].astype(BF16)
 
         @pl.when(core == 1)
         def _():
-            @pl.loop(0, WAVES // 2, unroll=8)
+            @pl.loop(0, HALF, unroll=8)
             def _(e):
-                base = (WAVES + e) * rows
-                for q in range(extra):
-                    first = stage[pl.ds(base + TILE * q, TILE), :]
-                    second = stage[pl.ds(base + rows // 2 + TILE * q, TILE), :]
-                    second = pltpu.roll(second, 64, 1)
-                    send[2 * e, main + q] = jnp.where(lane4 < 64, first, second).astype(BF16)
-                    send[2 * e + 1, main + q] = jnp.where(lane4 < 64, second, first).astype(BF16)
-
+                place = TILE * (WAVES + e)
+                for q, (one, two) in enumerate(pairs):
+                    first = stage[pl.ds(one * 512 + place, TILE), :]
+                    second = pltpu.roll(stage[pl.ds(two * 512 + place, TILE), :], 64, 1)
+                    q = len(tiles) + q
+                    send[2 * e, q] = jnp.where(lane4 < 64, first, second).astype(BF16)
+                    send[2 * e + 1, q] = jnp.where(lane4 < 64, second, first).astype(BF16)
+
+    hear(0)
+    say(1)
     state = recurrence_phase(0, cosine, state, alpha_ref, both_ref, tabs)
+    hear(1)
+    say(2)
     state = recurrence_phase(1, cosine, state, alpha_ref, both_ref, tabs)
+    hear(2)
+    say(3)
     pass_on(light_groups)
     recurrence_phase(2, cosine, state, alpha_ref, both_ref, tabs)
     own_copy().wait()
     gathered(light_groups)
     for r in range(HEAVY, ROWS):
         legendre_row(r)
-    pack(stage_l, send_fl, LIGHT, 3, 2)
-    pl.semaphore_wait(z_ready, 3)
-    send_all(fl, 3, 2)
+    pack(send_fl, LIGHT_TILES, LIGHT_PAIRS)
+    hear(3)
+    send_half(fl, 0, 3, 2)
+    send_half(fl, 1, 3, 2)
 
     pass_on(heavy_groups)
     gathered(heavy_groups)
     for r in range(HEAVY):
         legendre_row(r)
-    pack(stage_h, send_fh, HEAVY, 2, 1)
-    send_all(fh, 2, 1)
-
+    pack(send_fh, HEAVY_TILES, HEAVY_PAIRS)
+    send_half(fh, 0, 2, 1)
+    send_half(fh, 1, 2, 1)
+
+    column_orders(wo_ref, z, mt_ref)
     longitude_tables(mt_ref, cos_xj, sin_xj, cos_jx, sin_jx, even_ref)
 
     fields = pick_fields()
 
-    def unpack(recv, rows, main, extra):
-        @pl.loop(0, WAVES, unroll=8)
-        def _(d):
-            base = d * rows
-            for q in range(main):
-                flat0[pl.ds(base + TILE * q, TILE), :] = recv[d, q].astype(F32)
-
-        @pl.when(core == 1)
-        def _():
-            odd = me % 2 == 1
-
-            @pl.loop(0, WAVES, unroll=8)
-            def _(d):
-                base = d * rows
-                later = []
-                for q in reversed(range(extra)):
-                    here = recv[d, main + q].astype(F32)
-                    there = pltpu.roll(here, 64, 1)
-                    flat1[pl.ds(base + TILE * q, TILE), :] = jnp.where(odd, there, here)
-                    later.append((base + rows // 2 + TILE * q, jnp.where(odd, here, there)))
-                for place, value in reversed(later):
-                    flat1[pl.ds(place, TILE), :] = value
+    def unpack(recv, tiles, pairs):
+        odd = me % 2 == 1
+        for half in range(2):
+
+            @pl.loop(0, HALF, unroll=8)
+            def _(t):
+                for q, tile in enumerate(tiles):
+                    place = pl.ds(flat_row(tile, half) + TILE * t, TILE)
+                    flat0[place, :] = recv[peer(half, t), q].astype(F32)
+
+            @pl.when(core == 1)
+            def _():
+                @pl.loop(0, HALF, unroll=8)
+                def _(t):
+                    for q, (one, two) in enumerate(pairs):
+                        here = recv[peer(half, t), len(tiles) + q].astype(F32)
+                        there = pltpu.roll(here, 64, 1)
+                        place = pl.ds(flat_row(one, half) + TILE * t, TILE)
+                        flat1[place, :] = jnp.where(odd, there, here)
+                        if two != one:
+                            place = pl.ds(flat_row(two, half) + TILE * t, TILE)
+                            flat1[place, :] = jnp.where(odd, here, there)
 
     def build(first_row, count):
         @pl.loop(0, count // LANES)
         def _(b):
-            local = pl.ds(pl.multiple_of(b * LANES, LANES), LANES)
             rows = pl.ds(pl.multiple_of(first_row + b * LANES, LANES), LANES)
-            raw = jnp.concatenate([flat0[local, :], flat1[local, :]], axis=1).astype(BF16)
+            raw = jnp.concatenate([flat0[rows, :], flat1[rows, :]], axis=1).astype(BF16)
             picked = jnp.dot(raw, fields, preferred_element_type=F32)
             even = even_ref[rows, :]
             even = jnp.concatenate([even, even], axis=1)
@@ -432,12 +487,12 @@
                 evens = both * even
                 ref[rows, :] = jnp.concatenate([evens, both - evens], axis=1).astype(BF16)
 
-    light = pl.ds(0, LIGHT_COLS)
-    heavy = pl.ds(LIGHT_COLS, COLS - LIGHT_COLS)
+    heavy = pl.ds(0, HEAVY_COLS)
+    light = pl.ds(HEAVY_COLS, COLS - HEAVY_COLS)
 
     wait_all(fl, 3, 2)
-    unpack(recv_fl, LIGHT, 3, 2)
-    build(0, LIGHT_COLS)
+    unpack(recv_fl, LIGHT_TILES, LIGHT_PAIRS)
+    build(HEAVY_COLS, COLS - HEAVY_COLS)
 
     @pl.loop(0, XROWS // XBLK)
     def _(b):
@@ -446,8 +501,8 @@
         acc_s[rows, :] = jnp.dot(sin_xj[rows, light], x_im[light, :], preferred_element_type=F32)
 
     wait_all(fh, 2, 1)
-    unpack(recv_fh, HEAVY, 2, 1)
-    build(LIGHT_COLS, COLS - LIGHT_COLS)
+    unpack(recv_fh, HEAVY_TILES, HEAVY_PAIRS)
+    build(0, HEAVY_COLS)
 
     @pl.loop(0, XROWS // XBLK)
     def _(b):
@@ -478,66 +533,63 @@
     places = place_fluxes()
 
     def direct(first_row, count):
-        @pl.loop(0, count // LANES)
-        def _(b):
-            local = pl.ds(pl.multiple_of(b * LANES, LANES), LANES)
-            rows = pl.ds(pl.multiple_of(first_row + b * LANES, LANES), LANES)
-            c = jnp.dot(cos_jx[rows, :], h_c[...], preferred_element_type=F32)
-            s = jnp.dot(sin_jx[rows, :], h_s[...], preferred_element_type=F32)
-            even = even_ref[rows, :] > 0.5
-            c = jnp.where(even, c[:, :128], c[:, 128:])
-            s = jnp.where(even, s[:, :128], s[:, 128:])
-            back = jnp.dot(
-                jnp.concatenate([c, s], axis=1).astype(BF16), places, preferred_element_type=F32
-            )
-            flat0[local, :] = back[:, :LANES]
-            flat1[local, :] = back[:, LANES:]
-
-    def pack_back(send, rows, main, extra):
-        @pl.loop(0, WAVES, unroll=8)
-        def _(d):
-            base = d * rows
-            for q in range(main):
-                send[d, q] = flat0[pl.ds(base + TILE * q, TILE), :].astype(BF16)
+        rows = pl.ds(first_row, count)
+        c = jnp.dot(cos_jx[rows, :], h_c[...], preferred_element_type=F32)
+        s = jnp.dot(sin_jx[rows, :], h_s[...], preferred_element_type=F32)
+        even = even_ref[rows, :] > 0.5
+        c = jnp.where(even, c[:, :128], c[:, 128:])
+        s = jnp.where(even, s[:, :128], s[:, 128:])
+        back = jnp.dot(
+            jnp.concatenate([c, s], axis=1).astype(BF16), places, preferred_element_type=F32
+        )
+        flat0[rows, :] = back[:, :LANES]
+        flat1[rows, :] = back[:, LANES:]
+
+    def pack_back(send, half, tiles, pairs):
+        @pl.loop(0, HALF, unroll=8)
+        def _(t):
+            for q, tile in enumerate(tiles):
+                place = pl.ds(flat_row(tile, half) + TILE * t, TILE)
+                send[peer(half, t), q] = flat0[place, :].astype(BF16)
 
         @pl.when(core == 1)
         def _():
-            @pl.loop(0, WAVES, unroll=8)
-            def _(d):
-                base = d * rows
-                for q in range(extra):
-                    first = flat1[pl.ds(base + TILE * q, TILE), :]
-                    second = flat1[pl.ds(base + rows // 2 + TILE * q, TILE), :]
-                    send[d, main + q] = jnp.where(lane4 < 64, first, second).astype(BF16)
-
-    direct(LIGHT_COLS, COLS - LIGHT_COLS)
-    pack_back(send_bh, HEAVY, 2, 1)
-    send_all(bh, 2, 1)
-    direct(0, LIGHT_COLS)
-    pack_back(send_bl, LIGHT, 3, 2)
-    send_all(bl, 3, 2)
-
-    def unpack_back(recv, stage, rows, main, extra):
+            @pl.loop(0, HALF, unroll=8)
+            def _(t):
+                for q, (one, two) in enumerate(pairs):
+                    first = flat1[pl.ds(flat_row(one, half) + TILE * t, TILE), :]
+                    second = flat1[pl.ds(flat_row(two, half) + TILE * t, TILE), :]
+                    both = jnp.where(lane4 < 64, first, second).astype(BF16)
+                    send[peer(half, t), len(tiles) + q] = both
+
+    for half in range(2):
+        direct(half * 256, 256)
+        pack_back(send_bh, half, HEAVY_TILES, HEAVY_PAIRS)
+        send_half(bh, half, 2, 1)
+    for half in range(2):
+        direct(HEAVY_COLS + half * 384, 384)
+        pack_back(send_bl, half, LIGHT_TILES, LIGHT_PAIRS)
+        send_half(bl, half, 3, 2)
+
+    def unpack_back(recv, tiles, pairs):
         @pl.loop(0, WAVES, unroll=8)
         def _(w):
-            for q in range(main):
-                stage[pl.ds(w * rows + TILE * q, TILE), :] = recv[w, q].astype(F32)
+            for q, tile in enumerate(tiles):
+                stage[pl.ds(tile * 512 + TILE * w, TILE), :] = recv[w, q].astype(F32)
 
         @pl.when(core == 1)
         def _():
-            @pl.loop(0, WAVES // 2, unroll=8)
+            @pl.loop(0, HALF, unroll=8)
             def _(e):
-                base = (WAVES + e) * rows
-                later = []
-                for q in reversed(range(extra)):
-                    low = recv[2 * e, main + q].astype(F32)
-                    high = recv[2 * e + 1, main + q].astype(F32)
+                place = TILE * (WAVES + e)
+                for q, (one, two) in enumerate(pairs):
+                    low = recv[2 * e, len(tiles) + q].astype(F32)
+                    high = recv[2 * e + 1, len(tiles) + q].astype(F32)
                     first = jnp.where(lane4 < 64, low, pltpu.roll(high, 64, 1))
-                    second = jnp.where(lane4 < 64, pltpu.roll(low, 64, 1), high)
-                    stage[pl.ds(base + TILE * q, TILE), :] = first
-                    later.append((base + rows // 2 + TILE * q, second))
-                for place, value in reversed(later):
-                    stage[pl.ds(place, TILE), :] = value
+                    stage[pl.ds(one * 512 + place, TILE), :] = first
+                    if two != one:
+                        second = jnp.where(lane4 < 64, pltpu.roll(low, 64, 1), high)
+                        stage[pl.ds(two * 512 + place, TILE), :] = second
 
     def e1_copy(g):
         window = (slice(None), pl.ds(2 * g, 2), slice(None), pl.ds(0, WIDTHS[g]))
@@ -570,10 +622,7 @@
             order = wo_ref[me * ROWS + r]
             weight = jnp.where(order == 0, 1.0, 0.5)
             factor = jnp.where(order < cut, area * weight, 0.0)
-            if r < HEAVY:
-                back = stage_h[pl.ds(r, LANES, stride=HEAVY), :]
-            else:
-                back = stage_l[pl.ds(r - HEAVY, LANES, stride=LIGHT), :]
+            back = stage[pl.ds(r // TILE * 512 + r % TILE, LANES, stride=TILE), :]
             sums = lax.dot_general(
                 (back.T * factor).astype(BF16), table, (((1,), (1,)), ((), ())),
                 preferred_element_type=F32,
@@ -585,13 +634,13 @@
         e1_copy(g).start()
 
     wait_all(bh, 2, 1)
-    unpack_back(recv_bh, stage_h, HEAVY, 2, 1)
+    unpack_back(recv_bh, HEAVY_TILES, HEAVY_PAIRS)
     for g in heavy_groups:
         flux_rows(g)
     for g in heavy_groups:
         add_cores(g)
     wait_all(bl, 3, 2)
-    unpack_back(recv_bl, stage_l, LIGHT, 3, 2)
+    unpack_back(recv_bl, LIGHT_TILES, LIGHT_PAIRS)
     for g in light_groups:
         flux_rows(g)
     for g in light_groups:
@@ -610,19 +659,19 @@
 
 
 def on_device(spectra, wave_order, truncation):
-    by_peer = wave_order.reshape(WAVES, ROWS)
-    orders = jnp.concatenate(
-        [by_peer[:, HEAVY:].reshape(LIGHT_COLS), by_peer[:, :HEAVY].reshape(COLS - LIGHT_COLS), truncation]
-    ).reshape(2 * COLS // LANES, LANES)
+    anywhere = pl.BlockSpec(memory_space=pl.ANY)
     vmem = pl.BlockSpec(memory_space=pltpu.VMEM)
     dma = pltpu.SemaphoreType.DMA
     message = lambda tiles: pltpu.VMEM((WAVES, tiles, TILE, LANES), BF16)
     flux = pl.pallas_call(
         kernel,
         out_shape=jax.ShapeDtypeStruct((1, ROWS, 8, TOP), BF16),
-        in_specs=[pl.BlockSpec(memory_space=pltpu.SMEM), vmem, pl.BlockSpec(memory_space=pl.ANY)],
+        in_specs=[anywhere] * 3,
         out_specs=vmem,
         scratch_shapes=[
+            pltpu.SMEM((TOP,), jnp.int32),
+            pltpu.SMEM((TOP,), jnp.int32),
+            pltpu.VMEM((16, LANES), jnp.int32),
             pltpu.VMEM((10, ROWS_PAD, LANES), F32),
             pltpu.VMEM((10, ROWS_PAD, LANES), F32),
             pltpu.VMEM((8 * TAB_STRIDE[0], LANES), F32),
@@ -634,12 +683,11 @@
             pltpu.VMEM((COLS, XPAD), BF16),
             pltpu.VMEM((COLS, LANES), F32),
             pltpu.VMEM((LEVS, ROWS, 8, TOP), BF16),
-            pltpu.VMEM((LANES * LIGHT + 8, LANES), F32),
-            pltpu.VMEM((LANES * HEAVY + 8, LANES), F32),
+            pltpu.VMEM((LANES * ROWS, LANES), F32),
             message(5), message(3), message(5), message(3),
             message(5), message(3), message(5), message(3),
-            pltpu.VMEM((LIGHT_COLS + 8, LANES), F32),
-            pltpu.VMEM((LIGHT_COLS + 8, LANES), F32),
+            pltpu.VMEM((COLS, LANES), F32),
+            pltpu.VMEM((COLS, LANES), F32),
             pltpu.VMEM((COLS, 512), BF16),
             pltpu.VMEM((COLS, 512), BF16),
             pltpu.VMEM((XROWS, 512), F32),
@@ -650,7 +698,8 @@
             pltpu.VMEM((4, ROWS, 8, TOP), BF16),
             pltpu.VMEM((4, ROWS, 8, TOP), BF16),
             pltpu.VMEM((3, ROWS, 8, TOP), BF16),
-            pltpu.SemaphoreType.REGULAR,
+            dma((2,)),
+            pltpu.SemaphoreType.REGULAR((4,)),
             dma,
             dma((4, GROUPS)), dma((4, GROUPS)), dma((4, GROUPS)), dma((4, GROUPS)),
             dma, dma, dma, dma, dma, dma, dma, dma,
@@ -660,7 +709,7 @@
             collective_id=0, has_side_effects=True, vmem_limit_bytes=60 * 2**20
         ),
         name="flux_transform",
-    )(wave_order, orders, spectra)
+    )(wave_order, truncation, spectra)
     return flux.astype(F32)
 
 

time: 93.7 us -> 85.5 us (0.912)
  Pallas kernels: 89.1 us -> 83.3 us
  local copies, waits for them, and re-layouts: 1.65 us -> 0 us
    pallas_call x1, Pallas kernels: 89.1 us -> 83.3 us  [on_device(): pl.pallas_call(kernel, out_shape=jax.ShapeDtypeStruct((1, ROWS, 8, TOP),...]
    reshape x3 -> x0, local copies, waits for them, and re-layouts: 0.99 us -> none  [the longest x1 0.79 us: on_device(): by_peer = wave_order.reshape(WAVES, ROWS)]
where the time goes in v4:
time: 85.5 us; the launch traced here: 85.3 us
  Pallas kernels  83.3 us (97%)
  other arithmetic  1.95 us (2%)
    pallas_call x1, Pallas kernels, on_device(): pl.pallas_call(kernel, out_shape=jax.ShapeDtypeStruct((1, ROWS, 8, TOP),...  83.3 us
    convert_element_type x1, other arithmetic, on_device(): return flux.astype(F32)  1.95 us

profile of v4, /device:TPU:1, one launch (start us, length us, event | category | flops | bytes accessed | tf_op | source)
XLA Modules:
  0.0 85.3 jit_solution(9660267053967124467)
XLA Ops:
  0.0 83.3 %flux_transform.1 = bf16[1,20,8,1280]{3,2,1,0:T(8,128)(2,1)} custom-call(s32[1280]{0:T(1024)} %wo_hbm.1, s32[1280]{0:T(1024)} %trunc_hbm.1, bf16[1,20,8,1280]{3,2,1,0:T(8,128)(2,1)} %spec_ref.1), custom_call_target="tpu_custom_call" | custom-call | tf_op jit(solution)/shard_map/flux_transform/pallas_call | solution.py:666
  83.3 1.9 %convert_element_type.3 = f32[1,20,8,1280]{3,2,1,0:T(8,128)} convert(bf16[1,20,8,1280]{3,2,1,0:T(8,128)(2,1)} %flux_transform.1) | non-fusion elementwise | flops 204800 | bytes 1228800 | tf_op jit(solution)/shard_map/convert_element_type | solution.py:713

commit v5 on v4

--- a/solution.py
+++ b/solution.py
@@ -16,25 +16,23 @@
 LON = 2560
 ROWS = 20
 ROWS_PAD = 24
-HEAVY = 8
 WAVES = 64
 LEVS = 8
 LANES = 128
 RESCALE = 16
-GROUPS = ROWS // 2
-WIDTHS = tuple(TOP - LANES * g for g in range(GROUPS))
+GROUPS = ROWS // 4
+WIDTHS = tuple(TOP - 2 * LANES * g for g in range(GROUPS))
 TAB_LEN = (1280, 768, 256)
 TAB_STRIDE = (1288, 776, 264)
 COLS = WAVES * ROWS
-HEAVY_COLS = WAVES * HEAVY
+HEAVY_COLS = WAVES * 8
 XROWS = 672
 XPAD = 768
 XBLK = 224
 TILE = 4
-HEAVY_TILES = (0, 1)
-LIGHT_TILES = (2, 3, 4)
-HEAVY_PAIRS = ((0, 1),)
-LIGHT_PAIRS = ((2, 3), (4, 4))
+HEAVY = (0, 1)
+MID = (2, 3)
+LIGHT = (4,)
 HALF = WAVES // 2
 
 
@@ -230,11 +228,13 @@
     wo_ref, trunc_ref, mt_ref,
     alpha_ref, both_ref, tab0, tab1, tab2,
     cos_xj, sin_xj, cos_jx, sin_jx, even_ref,
-    gath, stage, send_fl, send_fh, recv_fl, recv_fh, send_bl, send_bh, recv_bl, recv_bh,
+    gath, stage,
+    send_fl, send_fm, send_fh, recv_fl, recv_fm, recv_fh,
+    send_bl, send_bm, send_bh, recv_bl, recv_bm, recv_bh,
     flat0, flat1, x_re, x_im, acc_c, acc_s, h_c, h_s,
     partial, e1_recv, e2_send, e2_recv,
     in_sem, ready, own_sem, g_send, g_recv, c_send, c_recv,
-    fl_ss, fl_rs, fh_ss, fh_rs, bl_ss, bl_rs, bh_ss, bh_rs,
+    f_ss, f_rs, b_ss, b_rs,
     e1_ss, e1_rs, e2_ss, e2_rs,
 ):
     me = lax.axis_index("wave")
@@ -290,14 +290,12 @@
     h_c[pl.ds(XROWS, XPAD - XROWS), :] = jnp.zeros((XPAD - XROWS, 256), BF16)
     h_s[pl.ds(XROWS, XPAD - XROWS), :] = jnp.zeros((XPAD - XROWS, 256), BF16)
 
+    state = recurrence_phase(0, cosine, state, alpha_ref, both_ref, tabs)
     pl.semaphore_wait(barrier, 9)
     say(0)
 
-    light_groups = tuple(range(HEAVY // 2, GROUPS))
-    heavy_groups = tuple(range(HEAVY // 2))
-
     def piece(ref, level, g):
-        return ref.at[level, pl.ds(2 * g, 2), :, pl.ds(0, WIDTHS[g])]
+        return ref.at[level, pl.ds(4 * g, 4), :, pl.ds(0, WIDTHS[g])]
 
     def own_copy():
         return pltpu.make_async_copy(spec_ref.at[0], gath.at[lev], own_sem)
@@ -327,13 +325,16 @@
             for i in range(4):
                 core_copy(i, g).wait()
 
-    for groups in (light_groups, heavy_groups):
+    for groups in (LIGHT, MID, HEAVY):
         for g in groups:
-            for i in range(1, 4):
+            for i in (2, 1, 3):
                 y_copy(i, g).start()
         for g in groups:
             core_copy(0, g).start()
-    own_copy().start()
+        if groups == LIGHT:
+            own_copy().start()
+            hear(0)
+            say(1)
 
     angles = half_angles(lat0)[0:1]
     lane = iota((1, LANES), 1)
@@ -345,7 +346,7 @@
     sign = jnp.where(iota((1, TOP), 1) % 2 == 0, 1.0, -1.0)
 
     def legendre_row(r):
-        width = WIDTHS[r // 2]
+        width = WIDTHS[r // 4]
         table = table_rows(tabs, r, width)
         coeff = gath[:, r, :, 0:width].astype(F32)
         both_signs = jnp.stack([coeff, coeff * sign[:, :width]], axis=1).reshape(LANES, width)
@@ -355,20 +356,20 @@
         fourier = fourier * jnp.where(order < cut, weight, 0.0)
         stage[pl.ds(r // TILE * 512 + r % TILE, LANES, stride=TILE), :] = fourier.T
 
-    def both_cores(main, extra, act):
+    def both_cores(tiles, act):
         @pl.when(core == 0)
         def _():
-            act(main)
+            act(len(tiles))
 
         @pl.when(core == 1)
         def _():
-            act(main + extra)
+            act(len(tiles) + 1)
 
     def peer(half, t):
         return lax.rem(z + 4 + 8 * half + t // 4, 16) * 4 + lax.rem(t, 4)
 
-    def send_half(bufs, half, main, extra):
-        send, recv, ss, rs = bufs
+    def send_half(bufs, half):
+        send, recv, ss, rs, tiles = bufs
 
         def start(count):
             @pl.loop(0, HALF, unroll=4)
@@ -382,26 +383,31 @@
                         device_id=(to, lev), device_id_type=MESH,
                     ).start()
 
-        both_cores(main, extra, start)
+        both_cores(tiles, start)
         if half == 1:
             recv[me] = send[me]
 
-    def wait_all(bufs, main, extra):
-        send, recv, ss, rs = bufs
+    def wait_all(bufs):
+        send, recv, ss, rs, tiles = bufs
 
         def wait(count):
             window = (pl.ds(0, WAVES - 1), pl.ds(0, count))
             pltpu.make_async_copy(send.at[window], send.at[window], ss).wait()
             pltpu.make_async_copy(recv.at[window], recv.at[window], rs).wait()
 
-        both_cores(main, extra, wait)
-
-    fl = (send_fl, recv_fl, fl_ss, fl_rs)
-    fh = (send_fh, recv_fh, fh_ss, fh_rs)
-    bl = (send_bl, recv_bl, bl_ss, bl_rs)
-    bh = (send_bh, recv_bh, bh_ss, bh_rs)
-
-    def pack(send, tiles, pairs):
+        both_cores(tiles, wait)
+
+    fl = (send_fl, recv_fl, f_ss.at[0], f_rs.at[0], LIGHT)
+    fm = (send_fm, recv_fm, f_ss.at[1], f_rs.at[1], MID)
+    fh = (send_fh, recv_fh, f_ss.at[2], f_rs.at[2], HEAVY)
+    bl = (send_bl, recv_bl, b_ss.at[0], b_rs.at[0], LIGHT)
+    bm = (send_bm, recv_bm, b_ss.at[1], b_rs.at[1], MID)
+    bh = (send_bh, recv_bh, b_ss.at[2], b_rs.at[2], HEAVY)
+
+    def pack(bufs):
+        send, tiles = bufs[0], bufs[4]
+        one, two = tiles[0], tiles[-1]
+
         @pl.loop(0, WAVES, unroll=8)
         def _(w):
             for q, tile in enumerate(tiles):
@@ -412,46 +418,42 @@
             @pl.loop(0, HALF, unroll=8)
             def _(e):
                 place = TILE * (WAVES + e)
-                for q, (one, two) in enumerate(pairs):
-                    first = stage[pl.ds(one * 512 + place, TILE), :]
-                    second = pltpu.roll(stage[pl.ds(two * 512 + place, TILE), :], 64, 1)
-                    q = len(tiles) + q
-                    send[2 * e, q] = jnp.where(lane4 < 64, first, second).astype(BF16)
-                    send[2 * e + 1, q] = jnp.where(lane4 < 64, second, first).astype(BF16)
-
-    hear(0)
-    say(1)
-    state = recurrence_phase(0, cosine, state, alpha_ref, both_ref, tabs)
+                q = len(tiles)
+                first = stage[pl.ds(one * 512 + place, TILE), :]
+                second = pltpu.roll(stage[pl.ds(two * 512 + place, TILE), :], 64, 1)
+                send[2 * e, q] = jnp.where(lane4 < 64, first, second).astype(BF16)
+                send[2 * e + 1, q] = jnp.where(lane4 < 64, second, first).astype(BF16)
+
     hear(1)
     say(2)
     state = recurrence_phase(1, cosine, state, alpha_ref, both_ref, tabs)
     hear(2)
     say(3)
-    pass_on(light_groups)
+    pass_on(LIGHT)
     recurrence_phase(2, cosine, state, alpha_ref, both_ref, tabs)
     own_copy().wait()
-    gathered(light_groups)
-    for r in range(HEAVY, ROWS):
-        legendre_row(r)
-    pack(send_fl, LIGHT_TILES, LIGHT_PAIRS)
-    hear(3)
-    send_half(fl, 0, 3, 2)
-    send_half(fl, 1, 3, 2)
-
-    pass_on(heavy_groups)
-    gathered(heavy_groups)
-    for r in range(HEAVY):
-        legendre_row(r)
-    pack(send_fh, HEAVY_TILES, HEAVY_PAIRS)
-    send_half(fh, 0, 2, 1)
-    send_half(fh, 1, 2, 1)
+    for bufs in (fl, fm, fh):
+        groups = bufs[4]
+        if groups != LIGHT:
+            pass_on(groups)
+        gathered(groups)
+        for g in groups:
+            for r in range(4 * g, 4 * g + 4):
+                legendre_row(r)
+        pack(bufs)
+        if groups == LIGHT:
+            hear(3)
+        send_half(bufs, 0)
+        send_half(bufs, 1)
 
     column_orders(wo_ref, z, mt_ref)
     longitude_tables(mt_ref, cos_xj, sin_xj, cos_jx, sin_jx, even_ref)
 
     fields = pick_fields()
 
-    def unpack(recv, tiles, pairs):
+    def unpack(bufs):
+        recv, tiles = bufs[1], bufs[4]
+        one, two = tiles[0], tiles[-1]
         odd = me % 2 == 1
         for half in range(2):
 
@@ -465,14 +467,13 @@
             def _():
                 @pl.loop(0, HALF, unroll=8)
                 def _(t):
-                    for q, (one, two) in enumerate(pairs):
-                        here = recv[peer(half, t), len(tiles) + q].astype(F32)
-                        there = pltpu.roll(here, 64, 1)
-                        place = pl.ds(flat_row(one, half) + TILE * t, TILE)
-                        flat1[place, :] = jnp.where(odd, there, here)
-                        if two != one:
-                            place = pl.ds(flat_row(two, half) + TILE * t, TILE)
-                            flat1[place, :] = jnp.where(odd, here, there)
+                    here = recv[peer(half, t), len(tiles)].astype(F32)
+                    there = pltpu.roll(here, 64, 1)
+                    place = pl.ds(flat_row(one, half) + TILE * t, TILE)
+                    flat1[place, :] = jnp.where(odd, there, here)
+                    if two != one:
+                        place = pl.ds(flat_row(two, half) + TILE * t, TILE)
+                        flat1[place, :] = jnp.where(odd, here, there)
 
     def build(first_row, count):
         @pl.loop(0, count // LANES)
@@ -490,8 +491,10 @@
     heavy = pl.ds(0, HEAVY_COLS)
     light = pl.ds(HEAVY_COLS, COLS - HEAVY_COLS)
 
-    wait_all(fl, 3, 2)
-    unpack(recv_fl, LIGHT_TILES, LIGHT_PAIRS)
+    wait_all(fl)
+    unpack(fl)
+    wait_all(fm)
+    unpack(fm)
     build(HEAVY_COLS, COLS - HEAVY_COLS)
 
     @pl.loop(0, XROWS // XBLK)
@@ -500,8 +503,8 @@
         acc_c[rows, :] = jnp.dot(cos_xj[rows, light], x_re[light, :], preferred_element_type=F32)
         acc_s[rows, :] = jnp.dot(sin_xj[rows, light], x_im[light, :], preferred_element_type=F32)
 
-    wait_all(fh, 2, 1)
-    unpack(recv_fh, HEAVY_TILES, HEAVY_PAIRS)
+    wait_all(fh)
+    unpack(fh)
     build(0, HEAVY_COLS)
 
     @pl.loop(0, XROWS // XBLK)
@@ -545,7 +548,10 @@
         flat0[rows, :] = back[:, :LANES]
         flat1[rows, :] = back[:, LANES:]
 
-    def pack_back(send, half, tiles, pairs):
+    def pack_back(bufs, half):
+        send, tiles = bufs[0], bufs[4]
+        one, two = tiles[0], tiles[-1]
+
         @pl.loop(0, HALF, unroll=8)
         def _(t):
             for q, tile in enumerate(tiles):
@@ -556,22 +562,27 @@
         def _():
             @pl.loop(0, HALF, unroll=8)
             def _(t):
-                for q, (one, two) in enumerate(pairs):
-                    first = flat1[pl.ds(flat_row(one, half) + TILE * t, TILE), :]
-                    second = flat1[pl.ds(flat_row(two, half) + TILE * t, TILE), :]
-                    both = jnp.where(lane4 < 64, first, second).astype(BF16)
-                    send[peer(half, t), len(tiles) + q] = both
+                first = flat1[pl.ds(flat_row(one, half) + TILE * t, TILE), :]
+                second = flat1[pl.ds(flat_row(two, half) + TILE * t, TILE), :]
+                both = jnp.where(lane4 < 64, first, second).astype(BF16)
+                send[peer(half, t), len(tiles)] = both
 
     for half in range(2):
         direct(half * 256, 256)
-        pack_back(send_bh, half, HEAVY_TILES, HEAVY_PAIRS)
-        send_half(bh, half, 2, 1)
+        pack_back(bh, half)
+        send_half(bh, half)
     for half in range(2):
         direct(HEAVY_COLS + half * 384, 384)
-        pack_back(send_bl, half, LIGHT_TILES, LIGHT_PAIRS)
-        send_half(bl, half, 3, 2)
-
-    def unpack_back(recv, tiles, pairs):
+        pack_back(bm, half)
+        send_half(bm, half)
+    for half in range(2):
+        pack_back(bl, half)
+        send_half(bl, half)
+
+    def unpack_back(bufs):
+        recv, tiles = bufs[1], bufs[4]
+        one, two = tiles[0], tiles[-1]
+
         @pl.loop(0, WAVES, unroll=8)
         def _(w):
             for q, tile in enumerate(tiles):
@@ -582,17 +593,16 @@
             @pl.loop(0, HALF, unroll=8)
             def _(e):
                 place = TILE * (WAVES + e)
-                for q, (one, two) in enumerate(pairs):
-                    low = recv[2 * e, len(tiles) + q].astype(F32)
-                    high = recv[2 * e + 1, len(tiles) + q].astype(F32)
-                    first = jnp.where(lane4 < 64, low, pltpu.roll(high, 64, 1))
-                    stage[pl.ds(one * 512 + place, TILE), :] = first
-                    if two != one:
-                        second = jnp.where(lane4 < 64, pltpu.roll(low, 64, 1), high)
-                        stage[pl.ds(two * 512 + place, TILE), :] = second
+                low = recv[2 * e, len(tiles)].astype(F32)
+                high = recv[2 * e + 1, len(tiles)].astype(F32)
+                first = jnp.where(lane4 < 64, low, pltpu.roll(high, 64, 1))
+                stage[pl.ds(one * 512 + place, TILE), :] = first
+                if two != one:
+                    second = jnp.where(lane4 < 64, pltpu.roll(low, 64, 1), high)
+                    stage[pl.ds(two * 512 + place, TILE), :] = second
 
     def e1_copy(g):
-        window = (slice(None), pl.ds(2 * g, 2), slice(None), pl.ds(0, WIDTHS[g]))
+        window = (slice(None), pl.ds(4 * g, 4), slice(None), pl.ds(0, WIDTHS[g]))
         return pltpu.make_async_remote_copy(
             partial.at[(1 - core,) + window], e1_recv.at[window], e1_ss.at[g], e1_rs.at[g],
             device_id=(me, partner), device_id_type=MESH,
@@ -607,7 +617,7 @@
 
     def add_cores(g):
         e1_copy(g).wait()
-        for r in (2 * g, 2 * g + 1):
+        for r in range(4 * g, 4 * g + 4):
             for q in range(4):
                 mine = partial[core, q, r, :, 0 : WIDTHS[g]].astype(F32)
                 other = e1_recv[q, r, :, 0 : WIDTHS[g]].astype(F32)
@@ -617,7 +627,7 @@
 
     def flux_rows(g):
         width = WIDTHS[g]
-        for r in (2 * g, 2 * g + 1):
+        for r in range(4 * g, 4 * g + 4):
             table = table_rows(tabs, r, width)
             order = wo_ref[me * ROWS + r]
             weight = jnp.where(order == 0, 1.0, 0.5)
@@ -633,29 +643,28 @@
                 partial[l % 2, l // 2, r, :, 0:width] = sums[l]
         e1_copy(g).start()
 
-    wait_all(bh, 2, 1)
-    unpack_back(recv_bh, HEAVY_TILES, HEAVY_PAIRS)
-    for g in heavy_groups:
-        flux_rows(g)
-    for g in heavy_groups:
-        add_cores(g)
-    wait_all(bl, 3, 2)
-    unpack_back(recv_bl, LIGHT_TILES, LIGHT_PAIRS)
-    for g in light_groups:
-        flux_rows(g)
-    for g in light_groups:
-        add_cores(g)
-    for g in range(GROUPS):
+    def finish(g):
         width = WIDTHS[g]
         for i in range(1, 4):
             e2_copy(i, g).wait()
-        for r in (2 * g, 2 * g + 1):
+        for r in range(4 * g, 4 * g + 4):
             total = e2_send[y, r, :, 0:width].astype(F32)
             for i in range(3):
                 total = total + e2_recv[i, r, :, 0:width].astype(F32)
             out_ref[0, r, :, 0:width] = total.astype(BF16)
             if width < TOP:
                 out_ref[0, r, :, width:TOP] = jnp.zeros((8, TOP - width), BF16)
+
+    for bufs in (bh, bm, bl):
+        groups = bufs[4]
+        wait_all(bufs)
+        unpack_back(bufs)
+        for g in groups:
+            flux_rows(g)
+        for g in groups:
+            add_cores(g)
+    for g in range(GROUPS):
+        finish(g)
 
 
 def on_device(spectra, wave_order, truncation):
@@ -684,8 +693,8 @@
             pltpu.VMEM((COLS, LANES), F32),
             pltpu.VMEM((LEVS, ROWS, 8, TOP), BF16),
             pltpu.VMEM((LANES * ROWS, LANES), F32),
-            message(5), message(3), message(5), message(3),
-            message(5), message(3), message(5), message(3),
+            message(2), message(3), message(3), message(2), message(3), message(3),
+            message(2), message(3), message(3), message(2), message(3), message(3),
             pltpu.VMEM((COLS, LANES), F32),
             pltpu.VMEM((COLS, LANES), F32),
             pltpu.VMEM((COLS, 512), BF16),
@@ -702,7 +711,7 @@
             pltpu.SemaphoreType.REGULAR((4,)),
             dma,
             dma((4, GROUPS)), dma((4, GROUPS)), dma((4, GROUPS)), dma((4, GROUPS)),
-            dma, dma, dma, dma, dma, dma, dma, dma,
+            dma((3,)), dma((3,)), dma((3,)), dma((3,)),
             dma((GROUPS,)), dma((GROUPS,)), dma((4, GROUPS)), dma((4, GROUPS)),
         ],
         compiler_params=pltpu.CompilerParams(

time: 85.5 us -> 83.1 us (0.972)
  Pallas kernels: 83.3 us -> 81 us
    pallas_call x1, Pallas kernels: 83.3 us -> 81 us  [on_device(): pl.pallas_call(kernel, out_shape=jax.ShapeDtypeStruct((1, ROWS, 8, TOP),...]
where the time goes in v5:
time: 83.1 us; the launch traced here: 82.9 us
  Pallas kernels  81 us (97%)
  other arithmetic  1.95 us (2%)
    pallas_call x1, Pallas kernels, on_device(): pl.pallas_call(kernel, out_shape=jax.ShapeDtypeStruct((1, ROWS, 8, TOP),...  81 us
    convert_element_type x1, other arithmetic, on_device(): return flux.astype(F32)  1.95 us

profile of v5, /device:TPU:1, one launch (start us, length us, event | category | flops | bytes accessed | tf_op | source)
XLA Modules:
  0.0 82.9 jit_solution(2137347273528695998)
XLA Ops:
  0.0 81.0 %flux_transform.1 = bf16[1,20,8,1280]{3,2,1,0:T(8,128)(2,1)} custom-call(s32[1280]{0:T(1024)} %wo_hbm.1, s32[1280]{0:T(1024)} %trunc_hbm.1, bf16[1,20,8,1280]{3,2,1,0:T(8,128)(2,1)} %spec_ref.1), custom_call_target="tpu_custom_call" | custom-call | tf_op jit(solution)/shard_map/flux_transform/pallas_call | solution.py:675
  81.0 1.9 %convert_element_type.3 = f32[1,20,8,1280]{3,2,1,0:T(8,128)} convert(bf16[1,20,8,1280]{3,2,1,0:T(8,128)(2,1)} %flux_transform.1) | non-fusion elementwise | flops 204800 | bytes 1228800 | tf_op jit(solution)/shard_map/convert_element_type | solution.py:722

commit v6 on v5

--- a/solution.py
+++ b/solution.py
@@ -683,16 +683,16 @@
             pltpu.VMEM((16, LANES), jnp.int32),
             pltpu.VMEM((10, ROWS_PAD, LANES), F32),
             pltpu.VMEM((10, ROWS_PAD, LANES), F32),
-            pltpu.VMEM((8 * TAB_STRIDE[0], LANES), F32),
-            pltpu.VMEM((8 * TAB_STRIDE[1], LANES), F32),
-            pltpu.VMEM((8 * TAB_STRIDE[2], LANES), F32),
+            pltpu.VMEM((9 * TAB_STRIDE[0], LANES), F32),
+            pltpu.VMEM((9 * TAB_STRIDE[1], LANES), F32),
+            pltpu.VMEM((9 * TAB_STRIDE[2], LANES), F32),
             pltpu.VMEM((XPAD, COLS), BF16),
             pltpu.VMEM((XPAD, COLS), BF16),
             pltpu.VMEM((COLS, XPAD), BF16),
             pltpu.VMEM((COLS, XPAD), BF16),
             pltpu.VMEM((COLS, LANES), F32),
             pltpu.VMEM((LEVS, ROWS, 8, TOP), BF16),
-            pltpu.VMEM((LANES * ROWS, LANES), F32),
+            pltpu.VMEM((LANES * ROWS + 8, LANES), F32),
             message(2), message(3), message(3), message(2), message(3), message(3),
             message(2), message(3), message(3), message(2), message(3), message(3),
             pltpu.VMEM((COLS, LANES), F32),

time: 83.1 us -> 83.1 us (level)
  no operation moved by 1% of the time
where the time goes in v6:
time: 83.1 us; the launch traced here: 82.9 us
  Pallas kernels  81 us (97%)
  other arithmetic  1.95 us (2%)
    pallas_call x1, Pallas kernels, on_device(): pl.pallas_call(kernel, out_shape=jax.ShapeDtypeStruct((1, ROWS, 8, TOP),...  81 us
    convert_element_type x1, other arithmetic, on_device(): return flux.astype(F32)  1.95 us

profile of v6, /device:TPU:1, one launch (start us, length us, event | category | flops | bytes accessed | tf_op | source)
XLA Modules:
  0.0 82.9 jit_solution(9878292944638993202)
XLA Ops:
  0.0 81.0 %flux_transform.1 = bf16[1,20,8,1280]{3,2,1,0:T(8,128)(2,1)} custom-call(s32[1280]{0:T(1024)} %wo_hbm.1, s32[1280]{0:T(1024)} %trunc_hbm.1, bf16[1,20,8,1280]{3,2,1,0:T(8,128)(2,1)} %spec_ref.1), custom_call_target="tpu_custom_call" | custom-call | tf_op jit(solution)/shard_map/flux_transform/pallas_call | solution.py:675
  81.0 1.9 %convert_element_type.3 = f32[1,20,8,1280]{3,2,1,0:T(8,128)} convert(bf16[1,20,8,1280]{3,2,1,0:T(8,128)(2,1)} %flux_transform.1) | non-fusion elementwise | flops 204800 | bytes 1228800 | tf_op jit(solution)/shard_map/convert_element_type | solution.py:722
